TPU v7x, 512 devices: a whole 4x8x8 slice. The times are simulated.
512 devices in a mesh: group: 16 (over x, z_hi), shard: 32 (over z_lo, y, core).
Axes of the slice: x: 4, y: 8, z: 8 (z_hi: 4, z_lo: 2; z = z_hi * 2 + z_lo), core: 2. Of those that a mesh axis runs over, the one named last changes fastest.
Arguments:
- user_shape: float32 [32768, 128], P(('group', 'shard')), may hold values from 1 to 10
- user_rate: float32 [32768, 128], P(('group', 'shard')), may hold values from 0.5 to 5
- item_shape: float32 [16384, 128], P('shard'), may hold values from 1 to 10
- item_rate: float32 [16384, 128], P('shard'), may hold values from 0.5 to 5
- tile_rows: int32 [65536], P(('group', 'shard')), may hold values from 0 to 15
- tile_cols: int32 [65536], P(('group', 'shard')), may hold values from 0 to 3
- clicks: bfloat16 [65536, 128, 128], P(('group', 'shard')), may hold values from 0 to 5, as said below
- tile_count: int32 [512], P(('group', 'shard')), may hold values from 16 to 128, as said below
Outputs:
- user_shape_new: float32 [32768, 128], P(('group', 'shard'))
- item_shape_new: float32 [16384, 128], P('shard')
Inputs may be any that keep to these rules, and one draw needn't show every extreme that they name: `clicks`: every count is a whole number 0 to 5; most are 0. `tile_count`: some device has all 128 slots live in every draw; a device's block pairs may repeat.
All inputs are finite; a program needn't handle non-finite values.
Results may differ from a plain program's by a relative error of at most 0.0028.
Values may be sent and summed in bfloat16 or wider, within the bound.
No kernel may reach another device: no remote copies, remote signals or barrier semaphores. Data moves between devices by JAX's collectives and lax.ppermute only.
A program may use at most 64 MiB of HBM per device.

v0:
```python
import jax
import jax.numpy as jnp
from jax import lax
from jax.sharding import PartitionSpec as P

BATCH = 8


prior_shape = 0.3


def factors(shape, rate):
    return jnp.exp(lax.digamma(shape) - jnp.log(rate)).astype(jnp.bfloat16)


def item_total(item_acc):
    return lax.psum(item_acc, "group")


def body(user_shape, user_rate, item_shape, item_rate, tile_rows, tile_cols, clicks, tile_count):
    comps = user_shape.shape[1]
    edge = clicks.shape[1]
    own_users = user_shape.shape[0]
    user_local = factors(user_shape, user_rate)
    item_factor = factors(item_shape, item_rate)
    gathered = lax.all_gather(user_local, "shard", axis=0, tiled=True)
    user_blocks = gathered.reshape(-1, edge, comps)
    item_blocks = item_factor.reshape(-1, edge, comps)
    live_count = tile_count[0]
    rounds = (live_count + BATCH - 1) // BATCH
    offsets = jnp.arange(BATCH, dtype=jnp.int32)

    def fetch(turn):
        slot_ids = turn * BATCH + offsets
        rows = tile_rows[slot_ids]
        cols = tile_cols[slot_ids]
        weight = (slot_ids < live_count).astype(jnp.float32)
        a_tiles = user_blocks[rows]
        b_tiles = item_blocks[cols]
        denom = jnp.einsum("tuk,tik->tui", a_tiles, b_tiles, preferred_element_type=jnp.float32)
        counts = clicks[slot_ids].astype(jnp.float32) * weight[:, None, None]
        ratio = (counts / denom).astype(jnp.bfloat16)
        return (rows, cols, a_tiles, b_tiles, ratio)

    def user_part(user_acc, rows, a_tiles, b_tiles, ratio):
        product = jnp.einsum("tui,tik->tuk", ratio, b_tiles, preferred_element_type=jnp.float32)
        return user_acc.at[rows].add(a_tiles.astype(jnp.float32) * product)

    def item_part(item_acc, cols, a_tiles, b_tiles, ratio):
        product = jnp.einsum("tui,tuk->tik", ratio, a_tiles, preferred_element_type=jnp.float32)
        return item_acc.at[cols].add(b_tiles.astype(jnp.float32) * product)

    user_zero = jnp.zeros(user_blocks.shape, jnp.float32)
    item_zero = jnp.zeros(item_blocks.shape, jnp.float32)

    def joint_turn(turn, carry):
        rows, cols, a_tiles, b_tiles, ratio = fetch(turn)
        return (
            user_part(carry[0], rows, a_tiles, b_tiles, ratio),
            item_part(carry[1], cols, a_tiles, b_tiles, ratio),
        )

    user_acc, item_acc = lax.fori_loop(0, rounds, joint_turn, (user_zero, item_zero))
    item_sum = item_total(item_acc)
    item_new = prior_shape + item_sum.reshape(-1, comps)
    user_terms = user_acc.reshape(-1, comps)
    summed = lax.psum(user_terms, "shard")
    mine = lax.dynamic_slice_in_dim(summed, lax.axis_index("shard") * own_users, own_users, 0)
    return (prior_shape + mine, item_new)


def solution(mesh):
    return jax.shard_map(
        body,
        mesh=mesh,
        in_specs=(
            P(("group", "shard"), None),
            P(("group", "shard"), None),
            P("shard", None),
            P("shard", None),
            P(("group", "shard")),
            P(("group", "shard")),
            P(("group", "shard"), None, None),
            P(("group", "shard")),
        ),
        out_specs=(P(("group", "shard"), None), P("shard", None)),
        check_vma=False,
    )
```

profile of v0, /device:TPU:1, one launch (start us, length us, event | category | flops | bytes accessed | tf_op | source)
XLA Modules:
  0.0 621.7 jit_solution(507488871245629464)
XLA Ops:
  8.9 38.5 %all_gather.3 = bf16[2048,128]{1,0:T(8,128)(2,1)S(1)} all-gather(bf16[64,128]{1,0:T(8,128)(2,1)S(1)} %fusion.16), channel_id=1, replica_groups=mesh['group'=16,'shard'=32] {'shard'}, dimensions={0}, use_global_device_ids=true | all-gather | bytes 540672 | tf_op jit(solution)/shard_map/all_gather | solution.py:26
  47.4 2.8 fusion.10
  50.4 164.1 %while.13 = (s32[]{:T(128)}, f32[16,128,128]{2,1,0:T(8,128)S(1)}, f32[4,128,128]{2,1,0:T(8,128)S(1)}, s32[]{:T(128)}, s32[128]{0:T(128)}, /*index=5*/bf16[16,128...) while((s32[]{:T(128)}, f32[16,128,128]{2,1,0:T(8,128)S(1)}, ...), condition=%wide.region_3.4_spmd.clone, body=%wide.region_0.3_spmd.clone.sunk | while | flops 101977192 | bytes 8401709 | solution.py:63
  51.1 1.3 gather_fusion.2
  52.4 1.3 gather_fusion
  55.0 2.8 gather_fusion.4
  59.6 1.0 scatter_fusion
  61.4 1.3 gather_fusion.2
  62.7 1.3 gather_fusion
  65.2 2.8 gather_fusion.4
  71.6 1.3 gather_fusion.2
  72.9 1.3 gather_fusion
  75.5 2.8 gather_fusion.4
  81.9 1.3 gather_fusion.2
  83.2 1.3 gather_fusion
  85.7 2.8 gather_fusion.4
  92.1 1.3 gather_fusion.2
  93.4 1.3 gather_fusion
  96.0 2.8 gather_fusion.4
  100.6 1.0 scatter_fusion
  102.4 1.3 gather_fusion.2
  103.7 1.3 gather_fusion
  106.2 2.8 gather_fusion.4
  112.6 1.3 gather_fusion.2
  113.9 1.3 gather_fusion
  116.5 2.8 gather_fusion.4
  122.9 1.3 gather_fusion.2
  124.2 1.3 gather_fusion
  126.7 2.8 gather_fusion.4
  133.1 1.3 gather_fusion.2
  134.5 1.3 gather_fusion
  137.0 2.8 gather_fusion.4
  141.7 1.0 scatter_fusion
  143.4 1.3 gather_fusion.2
  144.7 1.3 gather_fusion
  147.3 2.8 gather_fusion.4
  151.9 1.0 scatter_fusion
  153.7 1.3 gather_fusion.2
  155.0 1.3 gather_fusion
  157.5 2.8 gather_fusion.4
  162.2 1.0 scatter_fusion
  163.9 1.3 gather_fusion.2
  165.2 1.3 gather_fusion
  167.8 2.8 gather_fusion.4
  172.4 1.0 scatter_fusion
  174.2 1.3 gather_fusion.2
  175.5 1.3 gather_fusion
  178.0 2.8 gather_fusion.4
  182.7 1.0 scatter_fusion
  184.4 1.3 gather_fusion.2
  185.7 1.3 gather_fusion
  188.3 2.8 gather_fusion.4
  192.9 1.0 scatter_fusion
  194.7 1.3 gather_fusion.2
  196.0 1.3 gather_fusion
  198.5 2.8 gather_fusion.4
  203.2 1.0 scatter_fusion
  204.9 1.3 gather_fusion.2
  206.3 1.3 gather_fusion
  208.8 2.8 gather_fusion.4
  216.0 157.8 %all-reduce.5.cloned.1.call-done = f32[4,128,128]{2,1,0:T(8,128)} async-done(((f32[4,128,128]{2,1,0:T(8,128)}), f32[4,128,128]{2,1,0:T(8,128)}) %all-reduce.5.cloned.1.call-update) | async-done | bytes 262160 | tf_op jit(solution)/shard_map/psum | solution.py:17
  373.8 1.7 broadcast_add_fusion
  375.5 238.0 %all-reduce.3.cloned.1.call-done = f32[2048,128]{1,0:T(8,128)} async-done(((f32[2048,128]{1,0:T(8,128)}), f32[2048,128]{1,0:T(8,128)}) %all-reduce.3.cloned.1.call-update) | async-done | bytes 1048592 | tf_op jit(solution)/shard_map/psum | solution.py:67
  613.5 1.4 dynamic-slice_add_fusion
  (226 shorter events, 69.3 us)
Async XLA Ops:
  7.2 366.7 %all-reduce.5.cloned.1.call-start = ((), (), s32[]{:S(2)}) async-start(), calls=%async_computation.1 | async-start | bytes 524288 | tf_op jit(solution)/shard_map/psum | solution.py:17
  214.5 0.7 copy-start
  214.5 1.1 copy-start.1
  215.2 398.3 %all-reduce.3.cloned.1.call-start = ((), (), s32[]{:S(2)}) async-start(), calls=%async_computation | async-start | bytes 2097152 | tf_op jit(solution)/shard_map/psum | solution.py:67
Sparse Core Ops, SparseCore 0:
  215.4 158.4 all-reduce.4
  377.0 236.4 all-reduce.2
where the time goes:
time: 623 us; the launch traced here: 622 us
  waiting for transfers between devices  396 us (64%)
  local copies, waits for them, and re-layouts  106 us (17%)
  other arithmetic  51 us (8%)
  blocking collectives  38.5 us (6%)
  between operations  14.8 us (2%)
  matrix products  12.8 us (2%)
    psum x1, waiting for transfers between devices, body(): summed = lax.psum(user_terms, 'shard')  238 us
    psum x1, waiting for transfers between devices, item_total(): return lax.psum(item_acc, 'group')  158 us
    gather x16, local copies, waits for them, and re-layouts, fetch(): counts = clicks[slot_ids].astype(jnp.float32) * weight[:, None, None]  44.6 us
    all_gather x1, blocking collectives, body(): gathered = lax.all_gather(user_local, 'shard', axis=0, tiled=True)  38.5 us
    gather x16, local copies, waits for them, and re-layouts, fetch(): rows = tile_rows[slot_ids]  20.8 us
    gather x16, local copies, waits for them, and re-layouts, fetch(): cols = tile_cols[slot_ids]  20.8 us
    scatter-add x16, other arithmetic, user_part(): return user_acc.at[rows].add(a_tiles.astype(jnp.float32) * product)  16.6 us
    scatter-add x16, other arithmetic, item_part(): return item_acc.at[cols].add(b_tiles.astype(jnp.float32) * product)  16.5 us
  transfers between devices with their start and end apart: 2, of which 2 were waited for; matrix products, arithmetic and copies ran while one was open for 0% of the time, Pallas kernels for 0%

commit v1 on v0

v1 whole, which is shorter than its diff:
```python
import functools
import jax
import jax.numpy as jnp
from jax import lax
from jax.experimental import pallas as pl
from jax.experimental.pallas import tpu as pltpu
from jax.sharding import PartitionSpec as P

CHUNK = 16
STEP = 4

prior_shape = 0.3
f32 = jnp.float32
bf16 = jnp.bfloat16


def factors(shape, rate):
    return jnp.exp(lax.digamma(shape) - jnp.log(rate)).astype(bf16)


def add_clicks(slots, edge, rows_ref, cols_ref, count_ref, clicks_ref, out_ref, done_ref, total, held, sems):
    chunks = slots // CHUNK
    count = count_ref[0]

    def copy(c):
        part = pl.ds(c * CHUNK, CHUNK)
        return pltpu.make_async_copy(clicks_ref.at[part], held.at[part], sems.at[c])

    for c in range(chunks):
        @pl.when(c * CHUNK < count)
        def _():
            copy(c).start()

    def clear(r, carry):
        total[r] = jnp.zeros(total.shape[1:], f32)
        return carry

    lax.fori_loop(0, total.shape[0], clear, 0)

    def add(t, carry):
        row = rows_ref[t]
        cols = pl.ds(pl.multiple_of(cols_ref[t] * edge, edge), edge)
        total[row, :, cols] += held[t].astype(f32)
        return carry

    for c in range(chunks):
        @pl.when(c * CHUNK < count)
        def _():
            copy(c).wait()
            lax.fori_loop(c * CHUNK, jnp.minimum(count, (c + 1) * CHUNK), add, 0)

    def finish(r, carry):
        out_ref[r] = total[r].astype(bf16)
        return carry

    lax.fori_loop(0, total.shape[0], finish, 0)
    done_ref[...] = jnp.zeros_like(done_ref)


def pair_clicks(tile_rows, tile_cols, tile_count, clicks, user_blocks, item_blocks):
    slots, edge, _ = clicks.shape
    smem = pl.BlockSpec(memory_space=pltpu.SMEM)
    return pl.pallas_call(
        functools.partial(add_clicks, slots, edge),
        out_shape=(
            pltpu.VMEM((user_blocks, edge, item_blocks * edge), bf16),
            pltpu.VMEM((8, 128), f32),
        ),
        in_specs=[smem, smem, smem, pl.BlockSpec(memory_space=pltpu.HBM)],
        out_specs=(pl.BlockSpec(memory_space=pltpu.VMEM),) * 2,
        scratch_shapes=[
            pltpu.VMEM((user_blocks, edge, item_blocks * edge), f32),
            pltpu.VMEM((slots, edge, edge), bf16),
            pltpu.SemaphoreType.DMA((slots // CHUNK,)),
        ],
        compiler_params=pltpu.CompilerParams(vmem_limit_bytes=56 << 20),
        cost_estimate=pl.CostEstimate(flops=slots * edge * edge, bytes_accessed=2 * slots * edge * edge, transcendentals=0),
        name="pair_clicks",
    )(tile_rows, tile_cols, tile_count, clicks)


def half_terms(start_ref, a_ref, b_ref, counts_ref, user_ref, item_ref, total):
    blocks, half, comps = a_ref.shape
    rows = STEP * half
    first = pl.multiple_of(start_ref[0], half)
    b = b_ref[...]
    total[...] = jnp.zeros_like(total)

    def step(i, carry):
        at = pl.ds(i * STEP, STEP)
        a = a_ref[at].reshape(rows, comps)
        counts = counts_ref[at, pl.ds(first, half), :].reshape(rows, -1)
        denom = lax.dot_general(a, b, (((1,), (1,)), ((), ())), preferred_element_type=f32)
        ratio = (counts.astype(f32) / denom).astype(bf16)
        product = jnp.dot(ratio, b, preferred_element_type=f32)
        terms = a.astype(f32) * product
        user_ref[at] = terms.reshape(STEP, half, comps).astype(user_ref.dtype)
        total[...] += lax.dot_general(a, ratio, (((0,), (0,)), ((), ())), preferred_element_type=f32)
        return carry

    lax.fori_loop(0, blocks // STEP, step, 0)


def first_half(start_ref, a_ref, b_ref, counts_ref, done_ref, user_ref, item_ref, total):
    half_terms(start_ref, a_ref, b_ref, counts_ref, user_ref, item_ref, total)
    item_ref[...] = total[...]


def second_half(start_ref, a_ref, b_ref, counts_ref, before_ref, user_ref, item_ref, total):
    half_terms(start_ref, a_ref, b_ref, counts_ref, user_ref, item_ref, total)
    both = (before_ref[...] + total[...]).T
    item_ref[...] = (b_ref[...].astype(f32) * both).astype(item_ref.dtype)


def join_cores(z_ref, mine_ref, got_ref, keep_ref, send_ref):
    blocks = keep_ref.shape[0]
    kept = pl.ds(z_ref[0] * blocks, blocks)
    sent = pl.ds((1 - z_ref[0]) * blocks, blocks)
    keep_ref[...] = mine_ref[kept] + got_ref[kept].astype(f32)
    send_ref[...] = (mine_ref[sent] + got_ref[sent].astype(f32)).astype(bf16)


def join_chips(keep_ref, got_ref, out_ref):
    out_ref[...] = (keep_ref[...] + got_ref[...].astype(f32)).astype(bf16)


def sum_items(parts_ref, after_ref, out_ref):
    total = jnp.sum(parts_ref[...].astype(f32), 0)
    out_ref[...] = jnp.broadcast_to(total.astype(bf16)[None], out_ref.shape)


def sum_users(parts_ref, out_ref):
    out_ref[...] = prior_shape + jnp.sum(parts_ref[...].astype(f32), 0)


def small(kernel, name, out_shape, *operands, specs=None):
    vmem = pl.BlockSpec(memory_space=pltpu.VMEM)
    return pl.pallas_call(
        kernel,
        out_shape=out_shape,
        in_specs=specs or [vmem] * len(operands),
        out_specs=jax.tree.map(lambda _: vmem, out_shape),
        compiler_params=pltpu.CompilerParams(vmem_limit_bytes=8 << 20),
        name=name,
    )(*operands)


def run_half(kernel, name, start, a, b, counts, extra, user_type, item_shape, item_type):
    vmem = pl.BlockSpec(memory_space=pltpu.VMEM)
    blocks, half, comps = a.shape
    items = b.shape[0]
    return pl.pallas_call(
        kernel,
        out_shape=(
            pltpu.VMEM(a.shape, user_type),
            pltpu.VMEM(item_shape, item_type),
        ),
        in_specs=[pl.BlockSpec(memory_space=pltpu.SMEM)] + [vmem] * (3 + len(extra)),
        out_specs=(vmem, vmem),
        scratch_shapes=[pltpu.VMEM((comps, items), f32)],
        compiler_params=pltpu.CompilerParams(vmem_limit_bytes=16 << 20),
        cost_estimate=pl.CostEstimate(flops=6 * blocks * half * comps * items, bytes_accessed=4 * blocks * half * items, transcendentals=0),
        name=name,
    )(start, a, b, counts, *extra)


def body(n_group, n_shard, user_shape, user_rate, item_shape, item_rate, tile_rows, tile_cols, clicks, tile_count):
    own, comps = user_shape.shape
    items = item_shape.shape[0]
    edge = clicks.shape[1]
    chips = n_shard // 2
    swap = [(s, s ^ 1) for s in range(n_shard)]
    cross = [(s, s ^ chips) for s in range(n_shard)]
    same_core = [[2 * r + c for r in range(chips)] for c in range(2)]
    along_y = [[z * chips + 2 * y + c for y in range(chips // 2)] for z in range(2) for c in range(2)]
    place = lax.axis_index("shard")
    core = place & 1
    z = (place // chips).astype(jnp.int32).reshape(1)
    start = (core * own).astype(jnp.int32).reshape(1)

    def exchange(x):
        return lax.all_to_all(x, "shard", 0, 0, axis_index_groups=same_core)

    user_local = factors(user_shape, user_rate)
    a_mine = exchange(jnp.broadcast_to(user_local[None], (chips, own, comps)))
    b = factors(item_shape, item_rate)
    counts, done = pair_clicks(tile_rows, tile_cols, tile_count, clicks, chips, items // edge)
    a_mine, b, done = lax.optimization_barrier((a_mine, b, done))
    a_other = lax.ppermute(a_mine, "shard", swap)
    user_mine, item_part = run_half(first_half, "first_half", start, a_mine, b, counts, (done,), f32, (comps, items), f32)
    user_other, item_sum = run_half(second_half, "second_half", own - start, a_other, b, counts, (item_part,), bf16, (items, comps), bf16)

    user_sent = lax.ppermute(user_other, "shard", swap)
    item_parts = lax.all_to_all(item_sum.reshape(n_group, items // n_group, comps), "group", 0, 0)
    quarter = (chips // 2, own, comps)
    smem, vmem = pl.BlockSpec(memory_space=pltpu.SMEM), pl.BlockSpec(memory_space=pltpu.VMEM)
    keep, send = small(
        join_cores, "join_cores", (pltpu.VMEM(quarter, f32), pltpu.VMEM(quarter, bf16)), z, user_mine, user_sent,
        specs=[smem, vmem, vmem],
    )
    got = lax.ppermute(send, "shard", cross)
    item_piece = small(
        sum_items, "sum_items", jax.ShapeDtypeStruct(item_parts.shape, bf16), item_parts, send,
        specs=[vmem, pl.BlockSpec(memory_space=pl.ANY)],
    )
    item_all = lax.all_to_all(item_piece, "group", 0, 0)
    user_quad = small(join_chips, "join_chips", jax.ShapeDtypeStruct(quarter, bf16), keep, got)
    user_quad, item_all = lax.optimization_barrier((user_quad, item_all))
    user_parts = lax.all_to_all(user_quad, "shard", 0, 0, axis_index_groups=along_y)
    user_new = small(sum_users, "sum_users", jax.ShapeDtypeStruct((own, comps), f32), user_parts)
    item_new = prior_shape + item_all.reshape(items, comps).astype(f32)
    return user_new, item_new


def solution(mesh):
    return jax.shard_map(
        functools.partial(body, mesh.shape["group"], mesh.shape["shard"]),
        mesh=mesh,
        in_specs=(
            P(("group", "shard"), None),
            P(("group", "shard"), None),
            P("shard", None),
            P("shard", None),
            P(("group", "shard")),
            P(("group", "shard")),
            P(("group", "shard"), None, None),
            P(("group", "shard")),
        ),
        out_specs=(P(("group", "shard"), None), P("shard", None)),
        check_vma=False,
    )
```

time: 623 us -> 82.2 us (0.13)
  the two profiles are of different devices: /device:TPU:1 before, /device:TPU:8 now
where the time goes in v1:
time: 82.2 us; the launch traced here: 81.5 us
  starting transfers between devices  36.7 us (45%)
  waiting for transfers between devices  28.7 us (35%)
  Pallas kernels  10.2 us (12%)
  other arithmetic  3.7 us (5%)
  between operations  1.43 us (2%)
    all_to_all x1, starting transfers between devices, body(): lax.all_to_all(item_sum.reshape(n_group, items // n_group, comps), 'group...  12 us
    all_to_all x1, waiting for transfers between devices, body(): lax.all_to_all(item_sum.reshape(n_group, items // n_group, comps), 'group...  11 us
    all_to_all x1, starting transfers between devices, exchange(): return lax.all_to_all(x, 'shard', 0, 0, axis_index_groups=same_core)  9.37 us
    all_to_all x1, waiting for transfers between devices, body(): lax.all_to_all(user_quad, 'shard', 0, 0, axis_index_groups=along_y)  6.89 us
    all_to_all x1, starting transfers between devices, body(): lax.all_to_all(user_quad, 'shard', 0, 0, axis_index_groups=along_y)  4.41 us
    ppermute x1, waiting for transfers between devices, body(): got = lax.ppermute(send, 'shard', cross)  4.29 us
    pallas_call x2, Pallas kernels, run_half(): pl.pallas_call(kernel, out_shape=(pltpu.VMEM(a.shape, user_type), pltpu.V...  4.16 us
    pallas_call x1, Pallas kernels, pair_clicks(): pl.pallas_call(functools.partial(add_clicks, slots, edge), out_shape=(plt...  4.01 us
  transfers between devices with their start and end apart: 7, of which 5 were waited for; matrix products, arithmetic and copies ran while one was open for 3% of the time, Pallas kernels for 8%

profile of v1, /device:TPU:8, one launch (start us, length us, event | category | flops | bytes accessed | tf_op | source)
XLA Modules:
  0.0 81.5 jit_solution(18003642337018226521)
XLA Ops:
  0.6 0.0 copy-start
  0.6 0.0 copy-start.1
  0.7 1.1 %fusion.10 = bf16[64,128]{1,0:T(8,128)(2,1)S(1)} fusion(f32[64,128]{1,0:T(8,128)} %param.9, f32[64,128]{1,0:T(8,128)} %param.8), kind=kLoop, calls=%fused_computation.15 | loop fusion | flops 630784 | bytes 81920 | tf_op jit(solution)/shard_map/convert_element_type | solution.py:18
  1.7 0.8 broadcast_in_dim.2
  2.5 9.4 %all-to-all-start = ((bf16[16,64,128]{2,1,0:T(8,128)(2,1)}), bf16[16,64,128]{2,1,0:T(8,128)(2,1)S(1)}, u32[]{:S(2)}, u32[]{:S(2)}) async-start(bf16[16,64,128]{2,1,0:T(8,128)(2,1)} %broadcast_in_dim.2), calls=%async_computation | async-start | bytes 524288 | tf_op jit(solution)/shard_map/all_to_all | solution.py:182
  12.5 4.0 %pair_clicks.1 = (bf16[16,128,512]{2,1,0:T(8,128)(2,1)S(1)}, f32[8,128]{1,0:T(8,128)S(1)}) custom-call(s32[128]{0:T(128)} %rows_ref.1, s32[128]{0:T(128)} %cols_ref.1, s32[1]{0:T(128)S(6)} %copy.10.count_ref, bf16[128,128,128]{2,1,0:T(8,128)(2,1)} %clicks_ref.1), custom_call_target="tpu_custom_call" | custom-call | flops 2097152 | bytes 4194304 | tf_op jit(solution)/shard_map/pair_clicks/pallas_call | solution.py:63
  16.5 0.0 copy-done
  16.5 0.0 copy-done.1
  16.6 1.9 %fusion.4.b_ref = bf16[512,128]{1,0:T(8,128)(2,1)S(1)} fusion(f32[512,128]{1,0:T(8,128)S(1)} %copy-done, f32[512,128]{1,0:T(8,128)S(1)} %copy-done.1), kind=kLoop, calls=%fused_computation.6 | loop fusion | flops 5046272 | bytes 655360 | tf_op jit(solution)/shard_map/convert_element_type | solution.py:18
  18.5 3.5 %all-to-all-done.a_ref = bf16[16,64,128]{2,1,0:T(8,128)(2,1)S(1)} async-done(((bf16[16,64,128]{2,1,0:T(8,128)(2,1)}), bf16[16,64,128]{2,1,0:T(8,128)(2,1)S(1)}, u32[]{:S(2)}, u32[]{:S(2)}) %all-to-all-start) | async-done | bytes 262176 | tf_op jit(solution)/shard_map/all_to_all | solution.py:182
  21.9 1.9 %collective-permute-start = (bf16[16,64,128]{2,1,0:T(8,128)(2,1)S(1)}, bf16[16,64,128]{2,1,0:T(8,128)(2,1)S(1)}, u32[]{:S(2)}, u32[]{:S(2)}) collective-permute-start(bf16[16,64,128]{2,1,0:T(8,128)(2,1)S(1)} %all-to-all-done.a_ref), channel_id=1, source_target_pairs={{0,1},{1,0},{2,3},{3,2},{4,5},{5,4},{6,7},{7,6},{8,9},{9,8},{10,11... | collective-permute-start | bytes 786440 | tf_op jit(solution)/shard_map/ppermute | solution.py:189
  23.8 1.7 %first_half.1 = (f32[16,64,128]{2,1,0:T(8,128)S(1)}, f32[128,512]{1,0:T(8,128)S(1)}) custom-call(s32[1]{0:T(128)} %bitcast.1.start_ref, bf16[16,64,128]{2,1,0:T(8,128)(2,1)S(1)} %all-to-all-done.a_ref, bf16[512,128]{1,0:T(8,128)(2,1)S(1)} %fusion.4.b_ref, bf16[16,128,512]{2,1,0:T(8,128)(2,1)S(1)} %get-tuple-element.18.counts_ref, ...), custom_call_target="tpu_custom_call" | custom-call | flops 402653184 | bytes 2097152 | tf_op jit(solution)/shard_map/first_half/pallas_call | solution.py:152
  25.5 0.0 collective-permute-done.a_ref
  25.5 2.5 %second_half.1 = (bf16[16,64,128]{2,1,0:T(8,128)(2,1)S(1)}, bf16[512,128]{1,0:T(8,128)(2,1)}) custom-call(s32[1]{0:T(128)S(6)} %sub.16.start_ref, bf16[16,64,128]{2,1,0:T(8,128)(2,1)S(1)} %collective-permute-done.a_ref, bf16[512,128]{1,0:T(8,128)(2,1)S(1)} %fusion.4.b_ref, bf16[16,128,512]{2,1,0:T(8,128)(2,1)S(1)} %get-tuple-element.18.counts_ref, ...), custom_call_target="tpu_custom_call" | custom-call | flops 402653184 | bytes 2097152 | tf_op jit(solution)/shard_map/second_half/pallas_call | solution.py:152
  28.0 2.4 %collective-permute-start.1 = (bf16[16,64,128]{2,1,0:T(8,128)(2,1)S(1)}, bf16[16,64,128]{2,1,0:T(8,128)(2,1)S(1)}, u32[]{:S(2)}, u32[]{:S(2)}) collective-permute-start(bf16[16,64,128]{2,1,0:T(8,128)(2,1)S(1)} %get-tuple-element.22), channel_id=1, source_target_pairs={{0,1},{1,0},{2,3},{3,2},{4,5},{5,4},{6,7},{7,6},{8,9},{9,8},{10,11... | collective-permute-start | bytes 786440 | tf_op jit(solution)/shard_map/ppermute | solution.py:193
  30.4 12.0 %all-to-all-start.1 = ((bf16[16,32,128]{2,1,0:T(8,128)(2,1)}), bf16[16,32,128]{2,1,0:T(8,128)(2,1)S(1)}, u32[]{:S(2)}, u32[]{:S(2)}) async-start(bf16[16,32,128]{2,1,0:T(8,128)(2,1)} %bitcast.2), calls=%async_computation.1 | async-start | bytes 262144 | tf_op jit(solution)/shard_map/all_to_all | solution.py:194
  42.4 0.0 collective-permute-done.1.got_ref
  42.5 11.0 %all-to-all-done.1.parts_ref = bf16[16,32,128]{2,1,0:T(8,128)(2,1)S(1)} async-done(((bf16[16,32,128]{2,1,0:T(8,128)(2,1)}), bf16[16,32,128]{2,1,0:T(8,128)(2,1)S(1)}, u32[]{:S(2)}, u32[]{:S(2)}) %all-to-all-start.1) | async-done | bytes 131104 | tf_op jit(solution)/shard_map/all_to_all | solution.py:194
  53.5 0.7 sum_items.1
  54.2 3.5 %all-to-all-start.2 = ((bf16[16,32,128]{2,1,0:T(8,128)(2,1)}), bf16[16,32,128]{2,1,0:T(8,128)(2,1)S(1)}, u32[]{:S(2)}, u32[]{:S(2)}) async-start(bf16[16,32,128]{2,1,0:T(8,128)(2,1)} %sum_items.1), calls=%async_computation.2 | async-start | bytes 262144 | tf_op jit(solution)/shard_map/all_to_all | solution.py:206
  57.7 3.1 %collective-permute-start.2 = (bf16[8,64,128]{2,1,0:T(8,128)(2,1)S(1)}, bf16[8,64,128]{2,1,0:T(8,128)(2,1)S(1)}, u32[]{:S(2)}, u32[]{:S(2)}) collective-permute-start(bf16[8,64,128]{2,1,0:T(8,128)(2,1)S(1)} %get-tuple-element.24.after_ref), channel_id=1, source_target_pairs={{0,16},{1,17},{2,18},{3,19},{4,20},{5,21},{6,22},{7,23},{8,24},{9,... | collective-permute-start | bytes 393224 | tf_op jit(solution)/shard_map/ppermute | solution.py:201
  60.8 4.3 %collective-permute-done.2.got_ref = bf16[8,64,128]{2,1,0:T(8,128)(2,1)S(1)} collective-permute-done((bf16[8,64,128]{2,1,0:T(8,128)(2,1)S(1)}, bf16[8,64,128]{2,1,0:T(8,128)(2,1)S(1)}, u32[]{:S(2)}, u32[]{:S(2)}) %collective-permute-start.2) | collective-permute-done | bytes 131104 | tf_op jit(solution)/shard_map/ppermute | solution.py:201
  65.1 0.7 join_chips.1
  65.7 3.1 %all-to-all-done.2 = bf16[16,32,128]{2,1,0:T(8,128)(2,1)S(1)} async-done(((bf16[16,32,128]{2,1,0:T(8,128)(2,1)}), bf16[16,32,128]{2,1,0:T(8,128)(2,1)S(1)}, u32[]{:S(2)}, u32[]{:S(2)}) %all-to-all-start.2) | async-done | bytes 131104 | tf_op jit(solution)/shard_map/all_to_all | solution.py:206
  68.8 4.4 %all-to-all-start.3 = ((bf16[8,64,128]{2,1,0:T(8,128)(2,1)}), bf16[8,64,128]{2,1,0:T(8,128)(2,1)S(1)}, u32[]{:S(2)}, u32[]{:S(2)}) async-start(bf16[8,64,128]{2,1,0:T(8,128)(2,1)} %join_chips.1), calls=%async_computation.3 | async-start | bytes 262144 | tf_op jit(solution)/shard_map/all_to_all | solution.py:209
  73.2 0.7 convert_add_fusion
  74.0 6.9 %all-to-all-done.3.parts_ref = bf16[8,64,128]{2,1,0:T(8,128)(2,1)S(1)} async-done(((bf16[8,64,128]{2,1,0:T(8,128)(2,1)}), bf16[8,64,128]{2,1,0:T(8,128)(2,1)S(1)}, u32[]{:S(2)}, u32[]{:S(2)}) %all-to-all-start.3) | async-done | bytes 131104 | tf_op jit(solution)/shard_map/all_to_all | solution.py:209
  80.9 0.6 sum_users.1
  (1 shorter events, 0.0 us)
Async XLA Ops:
  0.6 15.9 %copy-start = (f32[512,128]{1,0:T(8,128)S(1)}, f32[512,128]{1,0:T(8,128)}, u32[]{:S(2)}) copy-start(f32[512,128]{1,0:T(8,128)} %param.11) | copy-start | bytes 786436
  0.6 15.9 %copy-start.1 = (f32[512,128]{1,0:T(8,128)S(1)}, f32[512,128]{1,0:T(8,128)}, u32[]{:S(2)}) copy-start(f32[512,128]{1,0:T(8,128)} %param.10) | copy-start | bytes 786436
  2.5 19.4 %all-to-all-start = ((bf16[16,64,128]{2,1,0:T(8,128)(2,1)}), bf16[16,64,128]{2,1,0:T(8,128)(2,1)S(1)}, u32[]{:S(2)}, u32[]{:S(2)}) async-start(bf16[16,64,128]{2,1,0:T(8,128)(2,1)} %broadcast_in_dim.2), calls=%async_computation | async-start | bytes 524288 | tf_op jit(solution)/shard_map/all_to_all | solution.py:182
  21.9 3.6 %collective-permute-start = (bf16[16,64,128]{2,1,0:T(8,128)(2,1)S(1)}, bf16[16,64,128]{2,1,0:T(8,128)(2,1)S(1)}, u32[]{:S(2)}, u32[]{:S(2)}) collective-permute-start(bf16[16,64,128]{2,1,0:T(8,128)(2,1)S(1)} %all-to-all-done.a_ref), channel_id=1, source_target_pairs={{0,1},{1,0},{2,3},{3,2},{4,5},{5,4},{6,7},{7,6},{8,9},{9,8},{10,11... | collective-permute-start | bytes 786440 | tf_op jit(solution)/shard_map/ppermute | solution.py:189
  28.0 14.4 %collective-permute-start.1 = (bf16[16,64,128]{2,1,0:T(8,128)(2,1)S(1)}, bf16[16,64,128]{2,1,0:T(8,128)(2,1)S(1)}, u32[]{:S(2)}, u32[]{:S(2)}) collective-permute-start(bf16[16,64,128]{2,1,0:T(8,128)(2,1)S(1)} %get-tuple-element.22), channel_id=1, source_target_pairs={{0,1},{1,0},{2,3},{3,2},{4,5},{5,4},{6,7},{7,6},{8,9},{9,8},{10,11... | collective-permute-start | bytes 786440 | tf_op jit(solution)/shard_map/ppermute | solution.py:193
  30.4 23.1 %all-to-all-start.1 = ((bf16[16,32,128]{2,1,0:T(8,128)(2,1)}), bf16[16,32,128]{2,1,0:T(8,128)(2,1)S(1)}, u32[]{:S(2)}, u32[]{:S(2)}) async-start(bf16[16,32,128]{2,1,0:T(8,128)(2,1)} %bitcast.2), calls=%async_computation.1 | async-start | bytes 262144 | tf_op jit(solution)/shard_map/all_to_all | solution.py:194
  54.2 14.7 %all-to-all-start.2 = ((bf16[16,32,128]{2,1,0:T(8,128)(2,1)}), bf16[16,32,128]{2,1,0:T(8,128)(2,1)S(1)}, u32[]{:S(2)}, u32[]{:S(2)}) async-start(bf16[16,32,128]{2,1,0:T(8,128)(2,1)} %sum_items.1), calls=%async_computation.2 | async-start | bytes 262144 | tf_op jit(solution)/shard_map/all_to_all | solution.py:206
  57.7 7.4 %collective-permute-start.2 = (bf16[8,64,128]{2,1,0:T(8,128)(2,1)S(1)}, bf16[8,64,128]{2,1,0:T(8,128)(2,1)S(1)}, u32[]{:S(2)}, u32[]{:S(2)}) collective-permute-start(bf16[8,64,128]{2,1,0:T(8,128)(2,1)S(1)} %get-tuple-element.24.after_ref), channel_id=1, source_target_pairs={{0,16},{1,17},{2,18},{3,19},{4,20},{5,21},{6,22},{7,23},{8,24},{9,... | collective-permute-start | bytes 393224 | tf_op jit(solution)/shard_map/ppermute | solution.py:201
  68.8 12.0 %all-to-all-start.3 = ((bf16[8,64,128]{2,1,0:T(8,128)(2,1)}), bf16[8,64,128]{2,1,0:T(8,128)(2,1)S(1)}, u32[]{:S(2)}, u32[]{:S(2)}) async-start(bf16[8,64,128]{2,1,0:T(8,128)(2,1)} %join_chips.1), calls=%async_computation.3 | async-start | bytes 262144 | tf_op jit(solution)/shard_map/all_to_all | solution.py:209

commit v2 on v1

v2 whole, which is shorter than its diff:
```python
import functools
import jax
import jax.numpy as jnp
from jax import lax
from jax.experimental import pallas as pl
from jax.experimental.pallas import tpu as pltpu
from jax.sharding import PartitionSpec as P

CHUNK = 16
STEP = 4

prior_shape = 0.3
f32 = jnp.float32
bf16 = jnp.bfloat16
ROWS = (((0,), (0,)), ((), ()))
LANES = (((1,), (1,)), ((), ()))


def factors(shape, rate):
    y = shape + 6.0
    u = shape * (shape + 5.0)
    below = (2.0 * shape + 5.0) * ((3.0 * u + 20.0) * u + 24.0) / (u * ((u + 10.0) * u + 24.0))
    w = 1.0 / y
    v = w * w
    tail = 0.5 * w + v * (1.0 / 12.0 - v * (1.0 / 120.0 - v * (1.0 / 252.0)))
    return (y / rate * jnp.exp(-(tail + below))).astype(bf16)


def user_copies(shape_ref, rate_ref, out_ref):
    out_ref[...] = jnp.broadcast_to(factors(shape_ref[...], rate_ref[...])[None], out_ref.shape)


def add_clicks(slots, edge, core_ref, rows_ref, cols_ref, count_ref, clicks_ref, shape_ref, rate_ref, kept_ref, sent_ref, factors_ref, total, held, sems):
    chunks = slots // CHUNK
    count = count_ref[0]
    blocks, _, items = total.shape
    half = kept_ref.shape[1]

    def copy(c):
        part = pl.ds(c * CHUNK, CHUNK)
        return pltpu.make_async_copy(clicks_ref.at[part], held.at[part], sems.at[c])

    for c in range(chunks):
        @pl.when(c * CHUNK < count)
        def _():
            copy(c).start()

    def clear(r, carry):
        total[r] = jnp.zeros(total.shape[1:], f32)
        return carry

    lax.fori_loop(0, blocks, clear, 0)
    wide = items // factors_ref.shape[1]
    for j in range(items // half):
        part = slice(j * half, (j + 1) * half)
        lanes = slice(j % wide * edge, (j % wide + 1) * edge)
        b = factors(shape_ref[part], rate_ref[part])
        factors_ref[part] = b
        sent_ref[blocks + j // wide, :, lanes] = b

    def add(t, carry):
        row = rows_ref[t]
        cols = pl.ds(pl.multiple_of(cols_ref[t] * edge, edge), edge)
        total[row, :, cols] += held[t].astype(f32)
        return carry

    for c in range(chunks):
        @pl.when(c * CHUNK < count)
        def _():
            copy(c).wait()
            lax.fori_loop(c * CHUNK, jnp.minimum(count, (c + 1) * CHUNK), add, 0)

    first = core_ref[0] * half
    kept = pl.ds(pl.multiple_of(first, half), half)
    sent = pl.ds(pl.multiple_of(half - first, half), half)

    def finish(r, carry):
        kept_ref[r] = total[r, kept, :].astype(bf16)
        sent_ref[r] = total[r, sent, :].astype(bf16)
        return carry

    lax.fori_loop(0, blocks, finish, 0)


def pair_clicks(core, tile_rows, tile_cols, tile_count, clicks, item_shape, item_rate, blocks):
    slots, edge, _ = clicks.shape
    items, comps = item_shape.shape
    half = edge // 2
    smem, vmem = pl.BlockSpec(memory_space=pltpu.SMEM), pl.BlockSpec(memory_space=pltpu.VMEM)
    return pl.pallas_call(
        functools.partial(add_clicks, slots, edge),
        out_shape=(
            pltpu.VMEM((blocks, half, items), bf16),
            pltpu.VMEM((blocks + comps // half, half, items), bf16),
            pltpu.VMEM((items, comps), bf16),
        ),
        in_specs=[smem] * 4 + [pl.BlockSpec(memory_space=pltpu.HBM), vmem, vmem],
        out_specs=(vmem,) * 3,
        scratch_shapes=[
            pltpu.VMEM((blocks, edge, items), f32),
            pltpu.VMEM((slots, edge, edge), bf16),
            pltpu.SemaphoreType.DMA((slots // CHUNK,)),
        ],
        compiler_params=pltpu.CompilerParams(vmem_limit_bytes=56 << 20),
        cost_estimate=pl.CostEstimate(flops=slots * edge * edge, bytes_accessed=2 * slots * edge * edge, transcendentals=0),
        name="pair_clicks",
    )(core, tile_rows, tile_cols, tile_count, clicks, item_shape, item_rate)


def add_terms(a_ref, counts_ref, b, add_users, total):
    blocks, half, comps = a_ref.shape
    rows = STEP * half
    total[...] = jnp.zeros_like(total)

    def step(i, carry):
        at = pl.ds(i * STEP, STEP)
        a = a_ref[at].reshape(rows, comps)
        denom = lax.dot_general(a, b, LANES, preferred_element_type=f32)
        ratio = (counts_ref[at].reshape(rows, -1).astype(f32) / denom).astype(bf16)
        product = jnp.dot(ratio, b, preferred_element_type=f32)
        add_users(at, (a.astype(f32) * product).reshape(STEP, half, comps))
        total[...] += lax.dot_general(a, ratio, ROWS, preferred_element_type=f32)
        return carry

    lax.fori_loop(0, blocks // STEP, step, 0)


def place_items(b, sums, out_ref, part, items_of):
    blocks = out_ref.shape[0]
    terms = (b.astype(f32) * sums.T).reshape(blocks, items_of, -1)
    out_ref[:, pl.ds(pl.multiple_of(part * items_of, items_of), items_of), :] = terms


def own_items(core_ref, a_ref, counts_ref, b_ref, user_ref, item_ref, total):
    b = b_ref[...]

    def add_users(at, terms):
        user_ref[at] = terms

    add_terms(a_ref, counts_ref, b, add_users, total)
    place_items(b, total[...], item_ref, core_ref[0], b.shape[0] // item_ref.shape[0])


def other_items(core_ref, a_ref, got_ref, user_ref, item_ref, keep_ref, send_ref, total, users, items):
    core = core_ref[0]
    blocks, half, comps = a_ref.shape
    b = jnp.concatenate(
        [
            got_ref[blocks + q, :, j : j + comps]
            for q in range(comps // half)
            for j in range(0, got_ref.shape[2], comps)
        ],
        0,
    )

    def add_users(at, terms):
        users[at] = user_ref[at] + terms

    add_terms(a_ref, got_ref, b, add_users, total)
    rows = b.shape[0] // blocks
    items[...] = item_ref[...]
    place_items(b, total[...], items, 1 - core, rows)

    @pl.when(core == 0)
    def _():
        keep_ref[...] = users[...]
        send_ref[...] = items[...].astype(bf16)

    @pl.when(core != 0)
    def _():
        keep_ref[...] = items[...]
        send_ref[...] = users[...].astype(bf16)


def assemble(core_ref, keep_ref, got_ref, out_ref):
    half = keep_ref.shape[1]

    @pl.when(core_ref[0] == 0)
    def _():
        out_ref[:, :half] = keep_ref[...].astype(bf16)
        out_ref[:, half:] = got_ref[...]

    @pl.when(core_ref[0] != 0)
    def _():
        total = keep_ref[...] + got_ref[...].astype(f32)
        rounded = total.astype(bf16)
        out_ref[:, :half] = rounded
        out_ref[:, half:] = (total - rounded.astype(f32)).astype(bf16)


def join(parts_ref, keep_ref, send_ref, items_ref):
    total = jnp.sum(parts_ref[...].astype(f32), 0)
    half = total.shape[0] // 2
    keep_ref[...] = prior_shape + total[:half]
    send_ref[...] = prior_shape + total[half:]
    pieces = (total[:half] + total[half:]).astype(bf16).reshape((2,) + items_ref.shape[2:])
    items_ref[...] = jnp.broadcast_to(pieces[None], items_ref.shape)


def small(kernel, out_shape, *operands, core=None, scratch=(), cost=None):
    vmem = pl.BlockSpec(memory_space=pltpu.VMEM)
    lead = () if core is None else (core,)
    return pl.pallas_call(
        kernel,
        out_shape=out_shape,
        in_specs=[pl.BlockSpec(memory_space=pltpu.SMEM)] * len(lead) + [vmem] * len(operands),
        out_specs=jax.tree.map(lambda _: vmem, out_shape),
        scratch_shapes=list(scratch),
        compiler_params=pltpu.CompilerParams(vmem_limit_bytes=24 << 20),
        cost_estimate=cost,
        name=kernel.__name__,
    )(*lead, *operands)


def body(n_group, n_shard, user_shape, user_rate, item_shape, item_rate, tile_rows, tile_cols, clicks, tile_count):
    own, comps = user_shape.shape
    items = item_shape.shape[0]
    edge = clicks.shape[1]
    chips = n_shard // 2
    both = ("group", "shard")
    swap = [(s, s ^ 1) for s in range(n_shard)]
    same_core = [[2 * r + c for r in range(chips)] for c in range(2)]
    users_or_items = [[g * n_shard + 2 * r for r in range(chips)] for g in range(n_group)]
    users_or_items += [[g * n_shard + 2 * r + 1 for g in range(n_group)] for r in range(chips)]
    same_chip = [[g * n_shard + 2 * r + c for g in range(n_group) for c in range(2)] for r in range(chips)]
    core = (lax.axis_index("shard") & 1).astype(jnp.int32).reshape(1)

    copies = small(user_copies, jax.ShapeDtypeStruct((chips, own, comps), bf16), user_shape, user_rate)
    a_mine = lax.all_to_all(copies, "shard", 0, 0, axis_index_groups=same_core)
    kept, sent, b = pair_clicks(core, tile_rows, tile_cols, tile_count, clicks, item_shape, item_rate, chips)
    other = lax.ppermute(sent, "shard", swap)
    whole = (chips, own, comps)
    total = pltpu.VMEM((comps, items), f32)
    cost = pl.CostEstimate(flops=1 << 34, bytes_accessed=1 << 24, transcendentals=0)
    users, item_sums = small(own_items, (pltpu.VMEM(whole, f32), pltpu.VMEM(whole, f32)), a_mine, kept, b, core=core, scratch=(total,), cost=cost)
    keep, send = small(
        other_items, (pltpu.VMEM(whole, f32), pltpu.VMEM(whole, bf16)), a_mine, other, users, item_sums,
        core=core, scratch=(total, pltpu.VMEM(whole, f32), pltpu.VMEM(whole, f32)),
    )
    got = lax.ppermute(send, "shard", swap)
    terms = small(assemble, jax.ShapeDtypeStruct((chips, edge, comps), bf16), keep, got, core=core)
    parts = lax.all_to_all(terms, both, 0, 0, axis_index_groups=users_or_items)
    piece = (2, items // n_group, comps)
    keep, send, pieces = small(
        join,
        (
            jax.ShapeDtypeStruct((own, comps), f32),
            jax.ShapeDtypeStruct((own, comps), f32),
            jax.ShapeDtypeStruct((n_group,) + piece, bf16),
        ),
        parts,
    )
    item_all = lax.all_to_all(pieces.reshape((2 * n_group,) + piece[1:]), both, 0, 0, axis_index_groups=same_chip)
    got = lax.ppermute(send, "shard", swap)
    user_new = jnp.where(core[0] == 0, keep, got)
    item_new = prior_shape + item_all.reshape((n_group,) + piece)[:, 1].reshape(items, comps).astype(f32)
    return user_new, item_new


def solution(mesh):
    return jax.shard_map(
        functools.partial(body, mesh.shape["group"], mesh.shape["shard"]),
        mesh=mesh,
        in_specs=(
            P(("group", "shard"), None),
            P(("group", "shard"), None),
            P("shard", None),
            P("shard", None),
            P(("group", "shard")),
            P(("group", "shard")),
            P(("group", "shard"), None, None),
            P(("group", "shard")),
        ),
        out_specs=(P(("group", "shard"), None), P("shard", None)),
        check_vma=False,
    )
```

time: 82.2 us -> 77.3 us (0.940)
  the two profiles are of different devices: /device:TPU:8 before, /device:TPU:1 now
where the time goes in v2:
time: 77.3 us; the launch traced here: 76.7 us
  blocking collectives  26.9 us (35%)
  starting transfers between devices  21.5 us (28%)
  waiting for transfers between devices  12.3 us (16%)
  Pallas kernels  9.57 us (12%)
  local copies, waits for them, and re-layouts  3.71 us (5%)
  between operations  1.38 us (2%)
  other arithmetic  1.35 us (2%)
    all_to_all x1, blocking collectives, body(): parts = lax.all_to_all(terms, both, 0, 0, axis_index_groups=users_or_items)  26.9 us
    all_to_all x1, starting transfers between devices, body(): a_mine = lax.all_to_all(copies, 'shard', 0, 0, axis_index_groups=same_core)  9.56 us
    all_to_all x1, waiting for transfers between devices, body(): lax.all_to_all(pieces.reshape((2 * n_group,) + piece[1:]), both, 0, 0, ax...  9.28 us
    ppermute x2, starting transfers between devices, body(): got = lax.ppermute(send, 'shard', swap)  6.15 us
    pallas_call x5, Pallas kernels, small(): pl.pallas_call(kernel, out_shape=out_shape, in_specs=[pl.BlockSpec(memory...  5.35 us
    pallas_call x1, Pallas kernels, pair_clicks(): pl.pallas_call(functools.partial(add_clicks, slots, edge), out_shape=(plt...  4.23 us
    unnamed x8, local copies, waits for them, and re-layouts  3.71 us
    all_to_all x1, starting transfers between devices, body(): lax.all_to_all(pieces.reshape((2 * n_group,) + piece[1:]), both, 0, 0, ax...  3.66 us
  transfers between devices with their start and end apart: 5, of which 4 were waited for; matrix products, arithmetic and copies ran while one was open for 1% of the time, Pallas kernels for 8%

profile of v2, /device:TPU:1, one launch (start us, length us, event | category | flops | bytes accessed | tf_op | source)
XLA Modules:
  0.0 76.7 jit_solution(16312486035581300297)
XLA Ops:
  0.6 0.0 copy-start
  0.6 0.7 copy-done
  1.4 0.0 copy-start.1
  1.4 0.8 copy-done.1
  2.1 0.8 user_copies.1
  2.9 9.6 %all-to-all-start = ((bf16[16,64,128]{2,1,0:T(8,128)(2,1)}), bf16[16,64,128]{2,1,0:T(8,128)(2,1)S(1)}, u32[]{:S(2)}, u32[]{:S(2)}) async-start(bf16[16,64,128]{2,1,0:T(8,128)(2,1)} %user_copies.1), calls=%async_computation | async-start | bytes 524288 | tf_op jit(solution)/shard_map/all_to_all | solution.py:229
  13.1 4.2 %pair_clicks.1 = (bf16[16,64,512]{2,1,0:T(8,128)(2,1)S(1)}, bf16[18,64,512]{2,1,0:T(8,128)(2,1)S(1)}, bf16[512,128]{1,0:T(8,128)(2,1)S(1)}) custom-call(s32[1]{0:T(128)} %bitcast.core_ref, s32[128]{0:T(128)} %rows_ref.1, s32[128]{0:T(128)} %cols_ref.1, s32[1]{0:T(128)S(6)} %copy.12.count_ref, bf16[128,128,128]{2,1,0:T(8,128)(2,1)} %clicks_ref.1, ...), custom_call_target="tpu_custom_call" | custom-call | flops 2097152 | bytes 4194304 | tf_op jit(solution)/shard_map/pair_clicks/pallas_call | solution.py:90
  17.4 0.0 copy-start.2
  17.4 1.0 %copy-done.2 = bf16[16,64,512]{2,1,0:T(8,128)(2,1)} copy-done((bf16[16,64,512]{2,1,0:T(8,128)(2,1)}, bf16[16,64,512]{2,1,0:T(8,128)(2,1)S(1)}, u32[]{:S(2)}) %copy-start.2) | copy-done | bytes 1048600
  18.4 2.2 %collective-permute-start = (bf16[18,64,512]{2,1,0:T(8,128)(2,1)S(1)}, bf16[18,64,512]{2,1,0:T(8,128)(2,1)S(1)}, u32[]{:S(2)}, u32[]{:S(2)}) collective-permute-start(bf16[18,64,512]{2,1,0:T(8,128)(2,1)S(1)} %get-tuple-element.12), channel_id=1, source_target_pairs={{0,1},{1,0},{2,3},{3,2},{4,5},{5,4},{6,7},{7,6},{8,9},{9,8},{10,11... | collective-permute-start | bytes 3538952 | tf_op jit(solution)/shard_map/ppermute | solution.py:231
  20.5 0.7 all-to-all-done.a_ref
  21.2 0.0 copy-start.3
  21.2 1.2 %copy-done.3 = bf16[16,64,512]{2,1,0:T(8,128)(2,1)S(1)} copy-done((bf16[16,64,512]{2,1,0:T(8,128)(2,1)S(1)}, bf16[16,64,512]{2,1,0:T(8,128)(2,1)}, u32[]{:S(2)}) %copy-start.3) | copy-done | bytes 1048600
  22.4 1.8 %own_items.1 = (f32[16,64,128]{2,1,0:T(8,128)S(1)}, f32[16,64,128]{2,1,0:T(8,128)S(1)}) custom-call(s32[1]{0:T(128)} %bitcast.core_ref, bf16[16,64,128]{2,1,0:T(8,128)(2,1)S(1)} %all-to-all-done.a_ref, bf16[16,64,512]{2,1,0:T(8,128)(2,1)S(1)} %copy-done.3, bf16[512,128]{1,0:T(8,128)(2,1)S(1)} %get-tuple-element.14.b_ref), custom_call_target="tpu_custom_call" | custom-call | flops 17179869184 | bytes 16777216 | tf_op jit(solution)/shard_map/own_items/pallas_call | solution.py:203
  24.3 0.0 collective-permute-done.got_ref
  24.3 1.9 %other_items.1 = (f32[16,64,128]{2,1,0:T(8,128)S(1)}, bf16[16,64,128]{2,1,0:T(8,128)(2,1)S(1)}) custom-call(s32[1]{0:T(128)} %bitcast.core_ref, bf16[16,64,128]{2,1,0:T(8,128)(2,1)S(1)} %all-to-all-done.a_ref, bf16[18,64,512]{2,1,0:T(8,128)(2,1)S(1)} %collective-permute-done.got_ref, f32[16,64,128]{2,1,0:T(8,128)S(1)} %get-tuple-element.15.user_ref, ...), custom_call_target="tpu_custom_call" | custom-call | tf_op jit(solution)/shard_map/other_items/pallas_call | solution.py:203
  26.2 4.2 %collective-permute-start.1 = (bf16[16,64,128]{2,1,0:T(8,128)(2,1)S(1)}, bf16[16,64,128]{2,1,0:T(8,128)(2,1)S(1)}, u32[]{:S(2)}, u32[]{:S(2)}) collective-permute-start(bf16[16,64,128]{2,1,0:T(8,128)(2,1)S(1)} %get-tuple-element.18), channel_id=1, source_target_pairs={{0,1},{1,0},{2,3},{3,2},{4,5},{5,4},{6,7},{7,6},{8,9},{9,8},{10,11... | collective-permute-start | bytes 786440 | tf_op jit(solution)/shard_map/ppermute | solution.py:240
  30.4 1.1 %collective-permute-done.1.got_ref = bf16[16,64,128]{2,1,0:T(8,128)(2,1)S(1)} collective-permute-done((bf16[16,64,128]{2,1,0:T(8,128)(2,1)S(1)}, bf16[16,64,128]{2,1,0:T(8,128)(2,1)S(1)}, u32[]{:S(2)}, u32[]{:S(2)}) %collective-permute-start.1) | collective-permute-done | bytes 262176 | tf_op jit(solution)/shard_map/ppermute | solution.py:240
  31.5 0.1 assemble.1
  31.6 26.9 %all_to_all.15.parts_ref = bf16[16,128,128]{2,1,0:T(8,128)(2,1)S(1)} all-to-all(bf16[16,128,128]{2,1,0:T(8,128)(2,1)S(1)} %assemble.1), channel_id=1, replica_groups={{0,2,4,6,8,10,12,14,16,18,20,22,24,26,28,30},{32,34,36,38,40,42,44,46,4..., dimensions={0} | all-to-all | bytes 1048576 | tf_op jit(solution)/shard_map/all_to_all | solution.py:242
  58.5 0.8 %join.1 = (f32[64,128]{1,0:T(8,128)S(1)}, f32[64,128]{1,0:T(8,128)S(1)}, bf16[16,2,32,128]{3,2,1,0:T(8,128)(2,1)}) custom-call(bf16[16,128,128]{2,1,0:T(8,128)(2,1)S(1)} %all_to_all.15.parts_ref), custom_call_target="tpu_custom_call" | custom-call | tf_op jit(solution)/shard_map/join/pallas_call | solution.py:203
  59.3 3.7 %all-to-all-start.2 = ((bf16[32,32,128]{2,1,0:T(8,128)(2,1)}), bf16[32,32,128]{2,1,0:T(8,128)(2,1)S(1)}, u32[]{:S(2)}, u32[]{:S(2)}) async-start(bf16[32,32,128]{2,1,0:T(8,128)(2,1)} %bitcast.1), calls=%async_computation.2 | async-start | bytes 524288 | tf_op jit(solution)/shard_map/all_to_all | solution.py:253
  62.9 1.9 %collective-permute-start.2 = (f32[64,128]{1,0:T(8,128)S(1)}, f32[64,128]{1,0:T(8,128)S(1)}, u32[]{:S(2)}, u32[]{:S(2)}) collective-permute-start(f32[64,128]{1,0:T(8,128)S(1)} %get-tuple-element.20), channel_id=1, source_target_pairs={{0,1},{1,0},{2,3},{3,2},{4,5},{5,4},{6,7},{7,6},{8,9},{9,8},{10,11... | collective-permute-start | bytes 98312 | tf_op jit(solution)/shard_map/ppermute | solution.py:254
  64.9 1.2 %collective-permute-done.2 = f32[64,128]{1,0:T(8,128)S(1)} collective-permute-done((f32[64,128]{1,0:T(8,128)S(1)}, f32[64,128]{1,0:T(8,128)S(1)}, u32[]{:S(2)}, u32[]{:S(2)}) %collective-permute-start.2) | collective-permute-done | bytes 32800 | tf_op jit(solution)/shard_map/ppermute | solution.py:254
  66.0 0.6 broadcast_select_fusion
  66.7 9.3 %all-to-all-done.2 = bf16[32,32,128]{2,1,0:T(8,128)(2,1)S(1)} async-done(((bf16[32,32,128]{2,1,0:T(8,128)(2,1)}), bf16[32,32,128]{2,1,0:T(8,128)(2,1)S(1)}, u32[]{:S(2)}, u32[]{:S(2)}) %all-to-all-start.2) | async-done | bytes 262176 | tf_op jit(solution)/shard_map/all_to_all | solution.py:253
  75.9 0.7 convert_add_fusion
Async XLA Ops:
  0.6 0.8 copy-start
  1.4 0.8 copy-start.1
  2.9 18.3 %all-to-all-start = ((bf16[16,64,128]{2,1,0:T(8,128)(2,1)}), bf16[16,64,128]{2,1,0:T(8,128)(2,1)S(1)}, u32[]{:S(2)}, u32[]{:S(2)}) async-start(bf16[16,64,128]{2,1,0:T(8,128)(2,1)} %user_copies.1), calls=%async_computation | async-start | bytes 524288 | tf_op jit(solution)/shard_map/all_to_all | solution.py:229
  17.4 1.0 %copy-start.2 = (bf16[16,64,512]{2,1,0:T(8,128)(2,1)}, bf16[16,64,512]{2,1,0:T(8,128)(2,1)S(1)}, u32[]{:S(2)}) copy-start(bf16[16,64,512]{2,1,0:T(8,128)(2,1)S(1)} %get-tuple-element.13.counts_ref) | copy-start | bytes 3145732
  18.4 5.9 %collective-permute-start = (bf16[18,64,512]{2,1,0:T(8,128)(2,1)S(1)}, bf16[18,64,512]{2,1,0:T(8,128)(2,1)S(1)}, u32[]{:S(2)}, u32[]{:S(2)}) collective-permute-start(bf16[18,64,512]{2,1,0:T(8,128)(2,1)S(1)} %get-tuple-element.12), channel_id=1, source_target_pairs={{0,1},{1,0},{2,3},{3,2},{4,5},{5,4},{6,7},{7,6},{8,9},{9,8},{10,11... | collective-permute-start | bytes 3538952 | tf_op jit(solution)/shard_map/ppermute | solution.py:231
  21.2 1.2 %copy-start.3 = (bf16[16,64,512]{2,1,0:T(8,128)(2,1)S(1)}, bf16[16,64,512]{2,1,0:T(8,128)(2,1)}, u32[]{:S(2)}) copy-start(bf16[16,64,512]{2,1,0:T(8,128)(2,1)} %copy-done.2) | copy-start | bytes 3145732
  26.2 5.4 %collective-permute-start.1 = (bf16[16,64,128]{2,1,0:T(8,128)(2,1)S(1)}, bf16[16,64,128]{2,1,0:T(8,128)(2,1)S(1)}, u32[]{:S(2)}, u32[]{:S(2)}) collective-permute-start(bf16[16,64,128]{2,1,0:T(8,128)(2,1)S(1)} %get-tuple-element.18), channel_id=1, source_target_pairs={{0,1},{1,0},{2,3},{3,2},{4,5},{5,4},{6,7},{7,6},{8,9},{9,8},{10,11... | collective-permute-start | bytes 786440 | tf_op jit(solution)/shard_map/ppermute | solution.py:240
  59.3 16.7 %all-to-all-start.2 = ((bf16[32,32,128]{2,1,0:T(8,128)(2,1)}), bf16[32,32,128]{2,1,0:T(8,128)(2,1)S(1)}, u32[]{:S(2)}, u32[]{:S(2)}) async-start(bf16[32,32,128]{2,1,0:T(8,128)(2,1)} %bitcast.1), calls=%async_computation.2 | async-start | bytes 524288 | tf_op jit(solution)/shard_map/all_to_all | solution.py:253
  62.9 3.1 %collective-permute-start.2 = (f32[64,128]{1,0:T(8,128)S(1)}, f32[64,128]{1,0:T(8,128)S(1)}, u32[]{:S(2)}, u32[]{:S(2)}) collective-permute-start(f32[64,128]{1,0:T(8,128)S(1)} %get-tuple-element.20), channel_id=1, source_target_pairs={{0,1},{1,0},{2,3},{3,2},{4,5},{5,4},{6,7},{7,6},{8,9},{9,8},{10,11... | collective-permute-start | bytes 98312 | tf_op jit(solution)/shard_map/ppermute | solution.py:254

commit v3 on v2

v3 whole, which is shorter than its diff:
```python
import functools
import jax
import jax.numpy as jnp
from jax import lax
from jax.experimental import pallas as pl
from jax.experimental.pallas import tpu as pltpu
from jax.sharding import PartitionSpec as P

CHUNK = 16
STEP = 4

prior_shape = 0.3
f32 = jnp.float32
bf16 = jnp.bfloat16
ROWS = (((0,), (0,)), ((), ()))
LANES = (((1,), (1,)), ((), ()))


def factors(shape, rate):
    y = shape + 6.0
    u = shape * (shape + 5.0)
    below = (2.0 * shape + 5.0) * ((3.0 * u + 20.0) * u + 24.0) / (u * ((u + 10.0) * u + 24.0))
    w = 1.0 / y
    v = w * w
    tail = 0.5 * w + v * (1.0 / 12.0 - v * (1.0 / 120.0 - v * (1.0 / 252.0)))
    return (y / rate * jnp.exp(-(tail + below))).astype(bf16)


def user_copies(shape_ref, rate_ref, out_ref):
    out_ref[...] = jnp.broadcast_to(factors(shape_ref[...], rate_ref[...])[None], out_ref.shape)


def add_clicks(slots, edge, core_ref, rows_ref, cols_ref, count_ref, clicks_ref, shape_ref, rate_ref, kept_ref, tail_ref, sent_ref, total, held, staged, sems):
    chunks = slots // CHUNK
    count = count_ref[0]
    blocks, _, items = total.shape
    half = staged.shape[1]
    near = kept_ref.shape[0]

    def copy(c):
        part = pl.ds(c * CHUNK, CHUNK)
        return pltpu.make_async_copy(clicks_ref.at[part], held.at[part], sems.at[c])

    for c in range(chunks):
        @pl.when(c * CHUNK < count)
        def _():
            copy(c).start()

    def clear(r, carry):
        total[r] = jnp.zeros(total.shape[1:], f32)
        return carry

    lax.fori_loop(0, blocks, clear, 0)
    wide = items // edge
    for j in range(items // half):
        part = slice(j * half, (j + 1) * half)
        lanes = slice(j % wide * edge, (j % wide + 1) * edge)
        sent_ref[blocks + j // wide, :, lanes] = factors(shape_ref[part], rate_ref[part])

    def add(t, carry):
        row = rows_ref[t]
        cols = pl.ds(pl.multiple_of(cols_ref[t] * edge, edge), edge)
        total[row, :, cols] += held[t].astype(f32)
        return carry

    for c in range(chunks):
        @pl.when(c * CHUNK < count)
        def _():
            copy(c).wait()
            lax.fori_loop(c * CHUNK, jnp.minimum(count, (c + 1) * CHUNK), add, 0)

    first = core_ref[0] * half
    kept = pl.ds(pl.multiple_of(first, half), half)
    sent = pl.ds(pl.multiple_of(half - first, half), half)

    def keep_tail(r, carry):
        staged[r] = total[near + r, kept, :].astype(bf16)
        return carry

    def keep(r, carry):
        kept_ref[r] = total[r, kept, :].astype(bf16)
        return carry

    def send(r, carry):
        sent_ref[r] = total[r, sent, :].astype(bf16)
        return carry

    lax.fori_loop(0, blocks - near, keep_tail, 0)
    out = pltpu.make_async_copy(staged, tail_ref, sems.at[chunks])
    out.start()
    lax.fori_loop(0, near, keep, 0)
    lax.fori_loop(0, blocks, send, 0)
    out.wait()


def pair_clicks(core, tile_rows, tile_cols, tile_count, clicks, item_shape, item_rate, blocks):
    slots, edge, _ = clicks.shape
    items, comps = item_shape.shape
    half = edge // 2
    smem, vmem = pl.BlockSpec(memory_space=pltpu.SMEM), pl.BlockSpec(memory_space=pltpu.VMEM)
    return pl.pallas_call(
        functools.partial(add_clicks, slots, edge),
        out_shape=(
            pltpu.VMEM((blocks - STEP, half, items), bf16),
            pltpu.HBM((STEP, half, items), bf16),
            pltpu.VMEM((blocks + comps // half, half, items), bf16),
        ),
        in_specs=[smem] * 4 + [pl.BlockSpec(memory_space=pltpu.HBM), vmem, vmem],
        out_specs=(vmem, pl.BlockSpec(memory_space=pltpu.HBM), vmem),
        scratch_shapes=[
            pltpu.VMEM((blocks, edge, items), f32),
            pltpu.VMEM((slots, edge, edge), bf16),
            pltpu.VMEM((STEP, half, items), bf16),
            pltpu.SemaphoreType.DMA((slots // CHUNK + 1,)),
        ],
        compiler_params=pltpu.CompilerParams(vmem_limit_bytes=56 << 20),
        cost_estimate=pl.CostEstimate(flops=slots * edge * edge, bytes_accessed=2 * slots * edge * edge, transcendentals=0),
        name="pair_clicks",
    )(core, tile_rows, tile_cols, tile_count, clicks, item_shape, item_rate)


def sent_factors(sent_ref, blocks, comps):
    return jnp.concatenate(
        [sent_ref[q, :, j : j + comps] for q in range(blocks, sent_ref.shape[0]) for j in range(0, sent_ref.shape[2], comps)],
        0,
    )


def add_terms(a_ref, counts_of, b, add_users, total):
    blocks, half, comps = a_ref.shape
    rows = STEP * half
    total[...] = jnp.zeros_like(total)
    for i in range(blocks // STEP):
        at = pl.ds(i * STEP, STEP)
        a = a_ref[at].reshape(rows, comps)
        denom = lax.dot_general(a, b, LANES, preferred_element_type=f32)
        ratio = (counts_of(i).reshape(rows, -1).astype(f32) / denom).astype(bf16)
        product = jnp.dot(ratio, b, preferred_element_type=f32)
        add_users(at, (a.astype(f32) * product).reshape(STEP, half, comps))
        total[...] += lax.dot_general(a, ratio, ROWS, preferred_element_type=f32)


def place_items(b, sums, out_ref, part, items_of):
    blocks = out_ref.shape[0]
    terms = (b.astype(f32) * sums.T).reshape(blocks, items_of, -1)
    out_ref[:, pl.ds(pl.multiple_of(part * items_of, items_of), items_of), :] = terms


def own_items(core_ref, a_ref, sent_ref, kept_ref, tail_ref, user_ref, item_ref, same_ref, total, held, sem):
    blocks, _, comps = a_ref.shape
    copy = pltpu.make_async_copy(tail_ref, held, sem)
    copy.start()
    b = sent_factors(sent_ref, blocks, comps)

    def counts_of(i):
        if (i + 1) * STEP <= kept_ref.shape[0]:
            return kept_ref[i * STEP : (i + 1) * STEP]
        copy.wait()
        return held[...]

    def add_users(at, terms):
        user_ref[at] = terms

    add_terms(a_ref, counts_of, b, add_users, total)
    place_items(b, total[...], item_ref, core_ref[0], b.shape[0] // blocks)


def near_items(core, a, sent, kept, tail):
    smem, vmem, hbm = (pl.BlockSpec(memory_space=m) for m in (pltpu.SMEM, pltpu.VMEM, pltpu.HBM))
    items = sent.shape[2]
    users, item_sums, _ = pl.pallas_call(
        own_items,
        out_shape=(pltpu.VMEM(a.shape, f32), pltpu.VMEM(a.shape, f32), pltpu.HBM(tail.shape, bf16)),
        in_specs=[smem, vmem, vmem, vmem, hbm],
        out_specs=(vmem, vmem, hbm),
        scratch_shapes=[pltpu.VMEM((a.shape[2], items), f32), pltpu.VMEM(tail.shape, bf16), pltpu.SemaphoreType.DMA],
        input_output_aliases={4: 2},
        compiler_params=pltpu.CompilerParams(vmem_limit_bytes=24 << 20),
        cost_estimate=pl.CostEstimate(flops=1 << 34, bytes_accessed=1 << 24, transcendentals=0),
        name="own_items",
    )(core, a, sent, kept, tail)
    return users, item_sums


def other_items(core_ref, a_ref, got_ref, user_ref, item_ref, keep_ref, send_ref, total, users, items):
    core = core_ref[0]
    blocks, half, comps = a_ref.shape
    b = sent_factors(got_ref, blocks, comps)

    def counts_of(i):
        return got_ref[i * STEP : (i + 1) * STEP]

    def add_users(at, terms):
        users[at] = user_ref[at] + terms

    add_terms(a_ref, counts_of, b, add_users, total)
    rows = b.shape[0] // blocks
    items[...] = item_ref[...]
    place_items(b, total[...], items, 1 - core, rows)

    @pl.when(core == 0)
    def _():
        keep_ref[...] = users[...]
        send_ref[...] = items[...].astype(bf16)

    @pl.when(core != 0)
    def _():
        keep_ref[...] = items[...]
        send_ref[...] = users[...].astype(bf16)


def first_terms(core_ref, keep_ref, got_ref, out_ref):
    other = jnp.where(core_ref[0] == 0, 0.0, got_ref[...].astype(f32))
    out_ref[...] = (keep_ref[...] + other).astype(bf16)


def second_terms(core_ref, parts_ref, got_ref, new_ref, out_ref):
    total = jnp.sum(parts_ref[...].astype(f32), 0)
    new_ref[...] = prior_shape + total

    @pl.when(core_ref[0] == 0)
    def _():
        out_ref[...] = got_ref[...]

    @pl.when(core_ref[0] != 0)
    def _():
        out_ref[...] = jnp.broadcast_to(total.astype(bf16)[None], out_ref.shape)


def last_terms(core_ref, parts_ref, out_ref):
    blocks, rows, _ = out_ref.shape

    @pl.when(core_ref[0] == 0)
    def _():
        new = prior_shape + jnp.sum(parts_ref[...].astype(f32), 0)
        rounded = new.astype(bf16)
        rest = (new - rounded.astype(f32)).astype(bf16)
        out_ref[...] = jnp.zeros_like(out_ref)
        for i in range(new.shape[0] // rows):
            part = slice(i * rows, (i + 1) * rows)
            out_ref[2 * i] = rounded[part]
            out_ref[2 * i + 1] = rest[part]

    @pl.when(core_ref[0] != 0)
    def _():
        out_ref[...] = parts_ref[:, :rows, :]


def finish(core_ref, new_ref, parts_ref, got_ref, user_ref, item_ref):
    blocks, rows, comps = got_ref.shape

    @pl.when(core_ref[0] == 0)
    def _():
        user_ref[...] = new_ref[...]
        item_ref[...] = prior_shape + got_ref[...].astype(f32).reshape(blocks * rows, comps)

    @pl.when(core_ref[0] != 0)
    def _():
        for i in range(user_ref.shape[0] // rows):
            user_ref[i * rows : (i + 1) * rows] = got_ref[2 * i].astype(f32) + got_ref[2 * i + 1].astype(f32)
        item_ref[...] = prior_shape + parts_ref[:, rows:, :].astype(f32).reshape(blocks * rows, comps)


def small(kernel, out_shape, *operands, core=None, scratch=(), limit=24):
    vmem = pl.BlockSpec(memory_space=pltpu.VMEM)
    lead = () if core is None else (core,)
    return pl.pallas_call(
        kernel,
        out_shape=out_shape,
        in_specs=[pl.BlockSpec(memory_space=pltpu.SMEM)] * len(lead) + [vmem] * len(operands),
        out_specs=jax.tree.map(lambda _: vmem, out_shape),
        scratch_shapes=list(scratch),
        compiler_params=pltpu.CompilerParams(vmem_limit_bytes=limit << 20),
        name=kernel.__name__,
    )(*lead, *operands)


def body(n_group, n_shard, user_shape, user_rate, item_shape, item_rate, tile_rows, tile_cols, clicks, tile_count):
    own, comps = user_shape.shape
    items = item_shape.shape[0]
    edge = clicks.shape[1]
    chips = n_shard // 2
    both = ("group", "shard")
    swap = [(s, s ^ 1) for s in range(n_shard)]
    same_core = [[2 * r + c for r in range(chips)] for c in range(2)]
    users_or_items = [[g * n_shard + 2 * r for r in range(chips)] for g in range(n_group)]
    users_or_items += [[g * n_shard + 2 * r + 1 for g in range(n_group)] for r in range(chips)]
    core = (lax.axis_index("shard") & 1).astype(jnp.int32).reshape(1)

    copies = small(user_copies, jax.ShapeDtypeStruct((chips, own, comps), bf16), user_shape, user_rate, limit=56)
    a_mine = lax.all_to_all(copies, "shard", 0, 0, axis_index_groups=same_core)
    kept, tail, sent = pair_clicks(core, tile_rows, tile_cols, tile_count, clicks, item_shape, item_rate, chips)
    other = lax.ppermute(sent, "shard", swap)
    whole = (chips, own, comps)
    total = pltpu.VMEM((comps, items), f32)
    users, item_sums = near_items(core, a_mine, sent, kept, tail)
    keep, send = small(
        other_items, (pltpu.VMEM(whole, f32), pltpu.VMEM(whole, bf16)), a_mine, other, users, item_sums,
        core=core, scratch=(total, pltpu.VMEM(whole, f32), pltpu.VMEM(whole, f32)),
    )
    got = lax.ppermute(send, "shard", swap)
    terms = small(first_terms, jax.ShapeDtypeStruct(whole, bf16), keep, got, core=core)
    parts = lax.all_to_all(terms, both, 0, 0, axis_index_groups=users_or_items)
    new, terms = small(
        second_terms, (jax.ShapeDtypeStruct((own, comps), f32), jax.ShapeDtypeStruct(whole, bf16)), parts, got, core=core
    )
    parts = lax.all_to_all(terms, both, 0, 0, axis_index_groups=users_or_items)
    last = small(last_terms, jax.ShapeDtypeStruct((n_group, items // n_group, comps), bf16), parts, core=core)
    got = lax.ppermute(last, "shard", swap)
    return small(
        finish, (jax.ShapeDtypeStruct((own, comps), f32), jax.ShapeDtypeStruct((items, comps), f32)), new, parts, got, core=core
    )


def solution(mesh):
    return jax.shard_map(
        functools.partial(body, mesh.shape["group"], mesh.shape["shard"]),
        mesh=mesh,
        in_specs=(
            P(("group", "shard"), None),
            P(("group", "shard"), None),
            P("shard", None),
            P("shard", None),
            P(("group", "shard")),
            P(("group", "shard")),
            P(("group", "shard"), None, None),
            P(("group", "shard")),
        ),
        out_specs=(P(("group", "shard"), None), P("shard", None)),
        check_vma=False,
    )
```

time: 77.3 us -> 71.7 us (0.928)
  blocking collectives: 26.9 us -> 37.6 us
  waiting for transfers between devices: 12.3 us -> 3.54 us
  local copies, waits for them, and re-layouts: 3.71 us -> 0 us
  starting transfers between devices: 21.5 us -> 19.1 us
  other arithmetic: 1.35 us -> 0 us
    all_to_all x1 -> x2, blocking collectives: 26.9 us -> 37.6 us  [body(): parts = lax.all_to_all(terms, both, 0, 0, axis_index_groups=users_or_items)]
    all_to_all x1 -> x0, waiting for transfers between devices: 9.28 us -> none  [body(): lax.all_to_all(pieces.reshape((2 * n_group,) + piece[1:]), both, 0, 0, ax...]
    unnamed x8 -> x0, local copies, waits for them, and re-layouts: 3.71 us -> none
    all_to_all x1 -> x0, starting transfers between devices: 3.66 us -> none  [body(): lax.all_to_all(pieces.reshape((2 * n_group,) + piece[1:]), both, 0, 0, ax...]
    pallas_call x0 -> x1, Pallas kernels: none -> 2.2 us  [near_items(): pl.pallas_call(own_items, out_shape=(pltpu.VMEM(a.shape, f32), pltpu.VMEM...]
    ppermute x2 -> x1, starting transfers between devices: 6.15 us -> 4.23 us  [body(): got = lax.ppermute(send, 'shard', swap)]
    ppermute x0 -> x1, starting transfers between devices: none -> 1.92 us  [body(): got = lax.ppermute(last, 'shard', swap)]
    pallas_call x5 -> x6, Pallas kernels: 5.35 us -> 3.76 us  [small(): pl.pallas_call(kernel, out_shape=out_shape, in_specs=[pl.BlockSpec(memory...]
  transfers between devices with their start and end apart: 5 -> 4, of which waited for: 4 -> 3; matrix products, arithmetic and copies ran while one was open for 1% -> 0% of each run, Pallas kernels for 8% -> 8%
where the time goes in v3:
time: 71.7 us; the launch traced here: 71.2 us
  blocking collectives  37.6 us (52%)
  starting transfers between devices  19.1 us (27%)
  Pallas kernels  9.56 us (13%)
  waiting for transfers between devices  3.54 us (5%)
  between operations  1.36 us (2%)
    all_to_all x2, blocking collectives, body(): parts = lax.all_to_all(terms, both, 0, 0, axis_index_groups=users_or_items)  37.6 us
    all_to_all x1, starting transfers between devices, body(): a_mine = lax.all_to_all(copies, 'shard', 0, 0, axis_index_groups=same_core)  9.56 us
    ppermute x1, starting transfers between devices, body(): got = lax.ppermute(send, 'shard', swap)  4.23 us
    pallas_call x6, Pallas kernels, small(): pl.pallas_call(kernel, out_shape=out_shape, in_specs=[pl.BlockSpec(memory...  3.76 us
    pallas_call x1, Pallas kernels, pair_clicks(): pl.pallas_call(functools.partial(add_clicks, slots, edge), out_shape=(plt...  3.59 us
    ppermute x1, starting transfers between devices, body(): other = lax.ppermute(sent, 'shard', swap)  3.39 us
    pallas_call x1, Pallas kernels, near_items(): pl.pallas_call(own_items, out_shape=(pltpu.VMEM(a.shape, f32), pltpu.VMEM...  2.2 us
    ppermute x1, starting transfers between devices, body(): got = lax.ppermute(last, 'shard', swap)  1.92 us
  transfers between devices with their start and end apart: 4, of which 3 were waited for; matrix products, arithmetic and copies ran while one was open for 0% of the time, Pallas kernels for 8%

profile of v3, /device:TPU:1, one launch (start us, length us, event | category | flops | bytes accessed | tf_op | source)
XLA Modules:
  0.0 71.2 jit_solution(17712388862102093033)
XLA Ops:
  0.6 1.5 %user_copies.1 = bf16[16,64,128]{2,1,0:T(8,128)(2,1)} custom-call(f32[64,128]{1,0:T(8,128)} %shape_ref.2, f32[64,128]{1,0:T(8,128)} %rate_ref.2), custom_call_target="tpu_custom_call" | custom-call | tf_op jit(solution)/shard_map/user_copies/pallas_call | solution.py:267
  2.2 9.6 %all-to-all-start = ((bf16[16,64,128]{2,1,0:T(8,128)(2,1)}), bf16[16,64,128]{2,1,0:T(8,128)(2,1)S(1)}, u32[]{:S(2)}, u32[]{:S(2)}) async-start(bf16[16,64,128]{2,1,0:T(8,128)(2,1)} %user_copies.1), calls=%async_computation | async-start | bytes 524288 | tf_op jit(solution)/shard_map/all_to_all | solution.py:291
  12.4 3.6 %pair_clicks.1 = (bf16[12,64,512]{2,1,0:T(8,128)(2,1)S(1)}, bf16[4,64,512]{2,1,0:T(8,128)(2,1)}, bf16[18,64,512]{2,1,0:T(8,128)(2,1)S(1)}) custom-call(s32[1]{0:T(128)} %bitcast.core_ref, s32[128]{0:T(128)} %rows_ref.1, s32[128]{0:T(128)} %cols_ref.1, s32[1]{0:T(128)S(6)} %copy.12.count_ref, bf16[128,128,128]{2,1,0:T(8,128)(2,1)} %clicks_ref.1, ...), custom_call_target="tpu_custom_call" | custom-call | flops 2097152 | bytes 4194304 | tf_op jit(solution)/shard_map/pair_clicks/pallas_call | solution.py:101
  16.0 3.4 %collective-permute-start = (bf16[18,64,512]{2,1,0:T(8,128)(2,1)S(1)}, bf16[18,64,512]{2,1,0:T(8,128)(2,1)S(1)}, u32[]{:S(2)}, u32[]{:S(2)}) collective-permute-start(bf16[18,64,512]{2,1,0:T(8,128)(2,1)S(1)} %get-tuple-element.11.sent_ref), channel_id=1, source_target_pairs={{0,1},{1,0},{2,3},{3,2},{4,5},{5,4},{6,7},{7,6},{8,9},{9,8},{10,11... | collective-permute-start | bytes 3538952 | tf_op jit(solution)/shard_map/ppermute | solution.py:293
  19.4 1.1 %all-to-all-done.a_ref = bf16[16,64,128]{2,1,0:T(8,128)(2,1)S(1)} async-done(((bf16[16,64,128]{2,1,0:T(8,128)(2,1)}), bf16[16,64,128]{2,1,0:T(8,128)(2,1)S(1)}, u32[]{:S(2)}, u32[]{:S(2)}) %all-to-all-start) | async-done | bytes 262176 | tf_op jit(solution)/shard_map/all_to_all | solution.py:291
  20.5 2.2 %own_items.1 = (f32[16,64,128]{2,1,0:T(8,128)S(1)}, f32[16,64,128]{2,1,0:T(8,128)S(1)}, bf16[4,64,512]{2,1,0:T(8,128)(2,1)}) custom-call(s32[1]{0:T(128)} %bitcast.core_ref, bf16[16,64,128]{2,1,0:T(8,128)(2,1)S(1)} %all-to-all-done.a_ref, bf16[18,64,512]{2,1,0:T(8,128)(2,1)S(1)} %get-tuple-element.11.sent_ref, ...), custom_call_target="tpu_custom_call", output_to_operand_aliasing={{2}: (4, {})} | custom-call | flops 17179869184 | bytes 16777216 | tf_op jit(solution)/shard_map/own_items/pallas_call | solution.py:171
  22.7 0.0 collective-permute-done.got_ref
  22.7 1.3 %other_items.1 = (f32[16,64,128]{2,1,0:T(8,128)S(1)}, bf16[16,64,128]{2,1,0:T(8,128)(2,1)S(1)}) custom-call(s32[1]{0:T(128)} %bitcast.core_ref, bf16[16,64,128]{2,1,0:T(8,128)(2,1)S(1)} %all-to-all-done.a_ref, bf16[18,64,512]{2,1,0:T(8,128)(2,1)S(1)} %collective-permute-done.got_ref, f32[16,64,128]{2,1,0:T(8,128)S(1)} %get-tuple-element.14.user_ref, ...), custom_call_target="tpu_custom_call" | custom-call | tf_op jit(solution)/shard_map/other_items/pallas_call | solution.py:267
  24.0 4.2 %collective-permute-start.1 = (bf16[16,64,128]{2,1,0:T(8,128)(2,1)S(1)}, bf16[16,64,128]{2,1,0:T(8,128)(2,1)S(1)}, u32[]{:S(2)}, u32[]{:S(2)}) collective-permute-start(bf16[16,64,128]{2,1,0:T(8,128)(2,1)S(1)} %get-tuple-element.17), channel_id=1, source_target_pairs={{0,1},{1,0},{2,3},{3,2},{4,5},{5,4},{6,7},{7,6},{8,9},{9,8},{10,11... | collective-permute-start | bytes 786440 | tf_op jit(solution)/shard_map/ppermute | solution.py:301
  28.3 1.1 %collective-permute-done.1.got_ref = bf16[16,64,128]{2,1,0:T(8,128)(2,1)S(1)} collective-permute-done((bf16[16,64,128]{2,1,0:T(8,128)(2,1)S(1)}, bf16[16,64,128]{2,1,0:T(8,128)(2,1)S(1)}, u32[]{:S(2)}, u32[]{:S(2)}) %collective-permute-start.1) | collective-permute-done | bytes 262176 | tf_op jit(solution)/shard_map/ppermute | solution.py:301
  29.4 0.1 first_terms.1
  29.5 23.6 %all_to_all.15.parts_ref = bf16[16,64,128]{2,1,0:T(8,128)(2,1)S(1)} all-to-all(bf16[16,64,128]{2,1,0:T(8,128)(2,1)S(1)} %first_terms.1), channel_id=1, replica_groups={{0,2,4,6,8,10,12,14,16,18,20,22,24,26,28,30},{32,34,36,38,40,42,44,46,4..., dimensions={0} | all-to-all | bytes 524288 | tf_op jit(solution)/shard_map/all_to_all | solution.py:303
  53.1 0.1 second_terms.1
  53.1 14.1 %all_to_all.16.parts_ref = bf16[16,64,128]{2,1,0:T(8,128)(2,1)S(1)} all-to-all(bf16[16,64,128]{2,1,0:T(8,128)(2,1)S(1)} %get-tuple-element.19), channel_id=1, replica_groups={{0,2,4,6,8,10,12,14,16,18,20,22,24,26,28,30},{32,34,36,38,40,42,44,46,4..., dimensions={0} | all-to-all | bytes 524288 | tf_op jit(solution)/shard_map/all_to_all | solution.py:307
  67.2 1.9 %collective-permute-start.2 = (bf16[16,32,128]{2,1,0:T(8,128)(2,1)S(1)}, bf16[16,32,128]{2,1,0:T(8,128)(2,1)S(1)}, u32[]{:S(2)}, u32[]{:S(2)}) collective-permute-start(bf16[16,32,128]{2,1,0:T(8,128)(2,1)S(1)} %last_terms.1), channel_id=1, source_target_pairs={{0,1},{1,0},{2,3},{3,2},{4,5},{5,4},{6,7},{7,6},{8,9},{9,8},{10,11... | collective-permute-start | bytes 393224 | tf_op jit(solution)/shard_map/ppermute | solution.py:309
  69.2 1.3 %collective-permute-done.2.got_ref = bf16[16,32,128]{2,1,0:T(8,128)(2,1)S(1)} collective-permute-done((bf16[16,32,128]{2,1,0:T(8,128)(2,1)S(1)}, bf16[16,32,128]{2,1,0:T(8,128)(2,1)S(1)}, u32[]{:S(2)}, u32[]{:S(2)}) %collective-permute-start.2) | collective-permute-done | bytes 131104 | tf_op jit(solution)/shard_map/ppermute | solution.py:309
  70.5 0.7 %finish.1 = (f32[64,128]{1,0:T(8,128)}, f32[512,128]{1,0:T(8,128)}) custom-call(s32[1]{0:T(128)} %bitcast.core_ref, f32[64,128]{1,0:T(8,128)S(1)} %get-tuple-element.18.new_ref, bf16[16,64,128]{2,1,0:T(8,128)(2,1)S(1)} %all_to_all.16.parts_ref, bf16[16,32,128]{2,1,0:T(8,128)(2,1)S(1)} %collective-permute-done.2.got_ref), custom_call_target="tpu_custom_call" | custom-call | tf_op jit(solution)/shard_map/finish/pallas_call | solution.py:267
  (1 shorter events, 0.0 us)
Async XLA Ops:
  2.2 18.3 %all-to-all-start = ((bf16[16,64,128]{2,1,0:T(8,128)(2,1)}), bf16[16,64,128]{2,1,0:T(8,128)(2,1)S(1)}, u32[]{:S(2)}, u32[]{:S(2)}) async-start(bf16[16,64,128]{2,1,0:T(8,128)(2,1)} %user_copies.1), calls=%async_computation | async-start | bytes 524288 | tf_op jit(solution)/shard_map/all_to_all | solution.py:291
  16.0 6.7 %collective-permute-start = (bf16[18,64,512]{2,1,0:T(8,128)(2,1)S(1)}, bf16[18,64,512]{2,1,0:T(8,128)(2,1)S(1)}, u32[]{:S(2)}, u32[]{:S(2)}) collective-permute-start(bf16[18,64,512]{2,1,0:T(8,128)(2,1)S(1)} %get-tuple-element.11.sent_ref), channel_id=1, source_target_pairs={{0,1},{1,0},{2,3},{3,2},{4,5},{5,4},{6,7},{7,6},{8,9},{9,8},{10,11... | collective-permute-start | bytes 3538952 | tf_op jit(solution)/shard_map/ppermute | solution.py:293
  24.0 5.4 %collective-permute-start.1 = (bf16[16,64,128]{2,1,0:T(8,128)(2,1)S(1)}, bf16[16,64,128]{2,1,0:T(8,128)(2,1)S(1)}, u32[]{:S(2)}, u32[]{:S(2)}) collective-permute-start(bf16[16,64,128]{2,1,0:T(8,128)(2,1)S(1)} %get-tuple-element.17), channel_id=1, source_target_pairs={{0,1},{1,0},{2,3},{3,2},{4,5},{5,4},{6,7},{7,6},{8,9},{9,8},{10,11... | collective-permute-start | bytes 786440 | tf_op jit(solution)/shard_map/ppermute | solution.py:301
  67.2 3.2 %collective-permute-start.2 = (bf16[16,32,128]{2,1,0:T(8,128)(2,1)S(1)}, bf16[16,32,128]{2,1,0:T(8,128)(2,1)S(1)}, u32[]{:S(2)}, u32[]{:S(2)}) collective-permute-start(bf16[16,32,128]{2,1,0:T(8,128)(2,1)S(1)} %last_terms.1), channel_id=1, source_target_pairs={{0,1},{1,0},{2,3},{3,2},{4,5},{5,4},{6,7},{7,6},{8,9},{9,8},{10,11... | collective-permute-start | bytes 393224 | tf_op jit(solution)/shard_map/ppermute | solution.py:309

commit v4 on v3

--- a/solution.py
+++ b/solution.py
@@ -153,9 +153,10 @@
     b = sent_factors(sent_ref, blocks, comps)
 
     def counts_of(i):
+        if (i + 1) * STEP == kept_ref.shape[0]:
+            copy.wait()
         if (i + 1) * STEP <= kept_ref.shape[0]:
             return kept_ref[i * STEP : (i + 1) * STEP]
-        copy.wait()
         return held[...]
 
     def add_users(at, terms):
@@ -209,56 +210,36 @@
         send_ref[...] = users[...].astype(bf16)
 
 
-def first_terms(core_ref, keep_ref, got_ref, out_ref):
-    other = jnp.where(core_ref[0] == 0, 0.0, got_ref[...].astype(f32))
+def first_terms(core_ref, keep_ref, sent_ref, out_ref):
+    other = jnp.where(core_ref[0] == 0, 0.0, sent_ref[0].astype(f32))
     out_ref[...] = (keep_ref[...] + other).astype(bf16)
 
 
-def second_terms(core_ref, parts_ref, got_ref, new_ref, out_ref):
+def second_terms(core_ref, parts_ref, sent_ref, new_ref, out_ref):
     total = jnp.sum(parts_ref[...].astype(f32), 0)
     new_ref[...] = prior_shape + total
 
     @pl.when(core_ref[0] == 0)
     def _():
-        out_ref[...] = got_ref[...]
+        out_ref[...] = sent_ref[1]
 
     @pl.when(core_ref[0] != 0)
     def _():
         out_ref[...] = jnp.broadcast_to(total.astype(bf16)[None], out_ref.shape)
 
 
-def last_terms(core_ref, parts_ref, out_ref):
-    blocks, rows, _ = out_ref.shape
+def finish(core_ref, new_ref, parts_ref, user_ref, item_ref):
+    rows = parts_ref.shape[2] // 2
 
     @pl.when(core_ref[0] == 0)
     def _():
-        new = prior_shape + jnp.sum(parts_ref[...].astype(f32), 0)
-        rounded = new.astype(bf16)
-        rest = (new - rounded.astype(f32)).astype(bf16)
-        out_ref[...] = jnp.zeros_like(out_ref)
-        for i in range(new.shape[0] // rows):
-            part = slice(i * rows, (i + 1) * rows)
-            out_ref[2 * i] = rounded[part]
-            out_ref[2 * i + 1] = rest[part]
+        user_ref[...] = new_ref[...]
+        item_ref[...] = prior_shape + parts_ref[1, :, :rows].astype(f32).reshape(item_ref.shape)
 
     @pl.when(core_ref[0] != 0)
     def _():
-        out_ref[...] = parts_ref[:, :rows, :]
-
-
-def finish(core_ref, new_ref, parts_ref, got_ref, user_ref, item_ref):
-    blocks, rows, comps = got_ref.shape
-
-    @pl.when(core_ref[0] == 0)
-    def _():
-        user_ref[...] = new_ref[...]
-        item_ref[...] = prior_shape + got_ref[...].astype(f32).reshape(blocks * rows, comps)
-
-    @pl.when(core_ref[0] != 0)
-    def _():
-        for i in range(user_ref.shape[0] // rows):
-            user_ref[i * rows : (i + 1) * rows] = got_ref[2 * i].astype(f32) + got_ref[2 * i + 1].astype(f32)
-        item_ref[...] = prior_shape + parts_ref[:, rows:, :].astype(f32).reshape(blocks * rows, comps)
+        user_ref[...] = prior_shape + jnp.sum(parts_ref[0].astype(f32), 0)
+        item_ref[...] = prior_shape + parts_ref[1, :, rows:].astype(f32).reshape(item_ref.shape)
 
 
 def small(kernel, out_shape, *operands, core=None, scratch=(), limit=24):
@@ -282,6 +263,7 @@
     chips = n_shard // 2
     both = ("group", "shard")
     swap = [(s, s ^ 1) for s in range(n_shard)]
+    pairs = [[2 * r, 2 * r + 1] for r in range(chips)]
     same_core = [[2 * r + c for r in range(chips)] for c in range(2)]
     users_or_items = [[g * n_shard + 2 * r for r in range(chips)] for g in range(n_group)]
     users_or_items += [[g * n_shard + 2 * r + 1 for g in range(n_group)] for r in range(chips)]
@@ -292,23 +274,21 @@
     kept, tail, sent = pair_clicks(core, tile_rows, tile_cols, tile_count, clicks, item_shape, item_rate, chips)
     other = lax.ppermute(sent, "shard", swap)
     whole = (chips, own, comps)
-    total = pltpu.VMEM((comps, items), f32)
     users, item_sums = near_items(core, a_mine, sent, kept, tail)
     keep, send = small(
         other_items, (pltpu.VMEM(whole, f32), pltpu.VMEM(whole, bf16)), a_mine, other, users, item_sums,
-        core=core, scratch=(total, pltpu.VMEM(whole, f32), pltpu.VMEM(whole, f32)),
-    )
-    got = lax.ppermute(send, "shard", swap)
-    terms = small(first_terms, jax.ShapeDtypeStruct(whole, bf16), keep, got, core=core)
+        core=core, scratch=(pltpu.VMEM((comps, items), f32), pltpu.VMEM(whole, f32), pltpu.VMEM(whole, f32)),
+    )
+    sent = lax.all_gather(send, "shard", axis_index_groups=pairs)
+    terms = small(first_terms, jax.ShapeDtypeStruct(whole, bf16), keep, sent, core=core)
     parts = lax.all_to_all(terms, both, 0, 0, axis_index_groups=users_or_items)
     new, terms = small(
-        second_terms, (jax.ShapeDtypeStruct((own, comps), f32), jax.ShapeDtypeStruct(whole, bf16)), parts, got, core=core
+        second_terms, (jax.ShapeDtypeStruct((own, comps), f32), jax.ShapeDtypeStruct(whole, bf16)), parts, sent, core=core
     )
     parts = lax.all_to_all(terms, both, 0, 0, axis_index_groups=users_or_items)
-    last = small(last_terms, jax.ShapeDtypeStruct((n_group, items // n_group, comps), bf16), parts, core=core)
-    got = lax.ppermute(last, "shard", swap)
+    parts = lax.all_gather(parts, "shard", axis_index_groups=pairs)
     return small(
-        finish, (jax.ShapeDtypeStruct((own, comps), f32), jax.ShapeDtypeStruct((items, comps), f32)), new, parts, got, core=core
+        finish, (jax.ShapeDtypeStruct((own, comps), f32), jax.ShapeDtypeStruct((items, comps), f32)), new, parts, core=core
     )
 
 

time: 71.7 us -> 68.6 us (0.957)
  starting transfers between devices: 19.1 us -> 13 us
  blocking collectives: 37.6 us -> 43.6 us
  waiting for transfers between devices: 3.54 us -> 0.86 us
    ppermute x2 -> x0, starting transfers between devices: 6.15 us -> none  [the longest x1 4.23 us: body(): got = lax.ppermute(send, 'shard', swap)]
    all_gather x0 -> x2, blocking collectives: none -> 6.07 us  [the longest x1 3.9 us: body(): sent = lax.all_gather(send, 'shard', axis_index_groups=pairs)]
    ppermute x2 -> x0, waiting for transfers between devices: 2.45 us -> none  [the longest x1 1.31 us: body(): got = lax.ppermute(last, 'shard', swap)]
    pallas_call x6 -> x5, Pallas kernels: 3.76 us -> 3.78 us  [small(): pl.pallas_call(kernel, out_shape=out_shape, in_specs=[pl.BlockSpec(memory...]
  transfers between devices with their start and end apart: 4 -> 2, of which waited for: 3 -> 2; matrix products, arithmetic and copies ran while one was open for 0% -> 0% of each run, Pallas kernels for 8% -> 8%
where the time goes in v4:
time: 68.6 us; the launch traced here: 68.1 us
  blocking collectives  43.6 us (64%)
  starting transfers between devices  13 us (19%)
  Pallas kernels  9.39 us (14%)
  between operations  1.33 us (2%)
  waiting for transfers between devices  0.86 us (1%)
    all_to_all x2, blocking collectives, body(): parts = lax.all_to_all(terms, both, 0, 0, axis_index_groups=users_or_items)  37.5 us
    all_to_all x1, starting transfers between devices, body(): a_mine = lax.all_to_all(copies, 'shard', 0, 0, axis_index_groups=same_core)  9.56 us
    pallas_call x1, Pallas kernels, pair_clicks(): pl.pallas_call(functools.partial(add_clicks, slots, edge), out_shape=(plt...  4.03 us
    all_gather x1, blocking collectives, body(): sent = lax.all_gather(send, 'shard', axis_index_groups=pairs)  3.9 us
    pallas_call x5, Pallas kernels, small(): pl.pallas_call(kernel, out_shape=out_shape, in_specs=[pl.BlockSpec(memory...  3.78 us
    ppermute x1, starting transfers between devices, body(): other = lax.ppermute(sent, 'shard', swap)  3.42 us
    all_gather x1, blocking collectives, body(): parts = lax.all_gather(parts, 'shard', axis_index_groups=pairs)  2.17 us
    pallas_call x1, Pallas kernels, near_items(): pl.pallas_call(own_items, out_shape=(pltpu.VMEM(a.shape, f32), pltpu.VMEM...  1.58 us
  transfers between devices with their start and end apart: 2, of which 2 were waited for; matrix products, arithmetic and copies ran while one was open for 0% of the time, Pallas kernels for 8%

profile of v4, /device:TPU:1, one launch (start us, length us, event | category | flops | bytes accessed | tf_op | source)
XLA Modules:
  0.0 68.1 jit_solution(9425758847046772152)
XLA Ops:
  0.6 1.5 %user_copies.1 = bf16[16,64,128]{2,1,0:T(8,128)(2,1)} custom-call(f32[64,128]{1,0:T(8,128)} %shape_ref.2, f32[64,128]{1,0:T(8,128)} %rate_ref.2), custom_call_target="tpu_custom_call" | custom-call | tf_op jit(solution)/shard_map/user_copies/pallas_call | solution.py:248
  2.2 9.6 %all-to-all-start = ((bf16[16,64,128]{2,1,0:T(8,128)(2,1)}), bf16[16,64,128]{2,1,0:T(8,128)(2,1)S(1)}, u32[]{:S(2)}, u32[]{:S(2)}) async-start(bf16[16,64,128]{2,1,0:T(8,128)(2,1)} %user_copies.1), calls=%async_computation | async-start | bytes 524288 | tf_op jit(solution)/shard_map/all_to_all | solution.py:273
  12.4 4.0 %pair_clicks.1 = (bf16[12,64,512]{2,1,0:T(8,128)(2,1)S(1)}, bf16[4,64,512]{2,1,0:T(8,128)(2,1)}, bf16[18,64,512]{2,1,0:T(8,128)(2,1)S(1)}) custom-call(s32[1]{0:T(128)} %bitcast.core_ref, s32[128]{0:T(128)} %rows_ref.1, s32[128]{0:T(128)} %cols_ref.1, s32[1]{0:T(128)S(6)} %copy.12.count_ref, bf16[128,128,128]{2,1,0:T(8,128)(2,1)} %clicks_ref.1, ...), custom_call_target="tpu_custom_call" | custom-call | flops 2097152 | bytes 4194304 | tf_op jit(solution)/shard_map/pair_clicks/pallas_call | solution.py:101
  16.4 3.4 %collective-permute-start = (bf16[18,64,512]{2,1,0:T(8,128)(2,1)S(1)}, bf16[18,64,512]{2,1,0:T(8,128)(2,1)S(1)}, u32[]{:S(2)}, u32[]{:S(2)}) collective-permute-start(bf16[18,64,512]{2,1,0:T(8,128)(2,1)S(1)} %get-tuple-element.11.sent_ref), channel_id=1, source_target_pairs={{0,1},{1,0},{2,3},{3,2},{4,5},{5,4},{6,7},{7,6},{8,9},{9,8},{10,11... | collective-permute-start | bytes 3538952 | tf_op jit(solution)/shard_map/ppermute | solution.py:275
  19.9 0.6 all-to-all-done.a_ref
  20.5 1.6 %own_items.1 = (f32[16,64,128]{2,1,0:T(8,128)S(1)}, f32[16,64,128]{2,1,0:T(8,128)S(1)}, bf16[4,64,512]{2,1,0:T(8,128)(2,1)}) custom-call(s32[1]{0:T(128)} %bitcast.core_ref, bf16[16,64,128]{2,1,0:T(8,128)(2,1)S(1)} %all-to-all-done.a_ref, bf16[18,64,512]{2,1,0:T(8,128)(2,1)S(1)} %get-tuple-element.11.sent_ref, ...), custom_call_target="tpu_custom_call", output_to_operand_aliasing={{2}: (4, {})} | custom-call | flops 17179869184 | bytes 16777216 | tf_op jit(solution)/shard_map/own_items/pallas_call | solution.py:172
  22.1 0.2 collective-permute-done.got_ref
  22.3 1.3 %other_items.1 = (f32[16,64,128]{2,1,0:T(8,128)S(1)}, bf16[16,64,128]{2,1,0:T(8,128)(2,1)S(1)}) custom-call(s32[1]{0:T(128)} %bitcast.core_ref, bf16[16,64,128]{2,1,0:T(8,128)(2,1)S(1)} %all-to-all-done.a_ref, bf16[18,64,512]{2,1,0:T(8,128)(2,1)S(1)} %collective-permute-done.got_ref, f32[16,64,128]{2,1,0:T(8,128)S(1)} %get-tuple-element.14.user_ref, ...), custom_call_target="tpu_custom_call" | custom-call | tf_op jit(solution)/shard_map/other_items/pallas_call | solution.py:248
  23.7 3.9 %all-gather = bf16[32,64,128]{2,1,0:T(8,128)(2,1)S(1)} all-gather(bf16[16,64,128]{2,1,0:T(8,128)(2,1)S(1)} %get-tuple-element.17), channel_id=2, replica_groups={{0,1},{2,3},{4,5},{6,7},{8,9},{10,11},{12,13},{14,15},{16,17},{18,19},{..., dimensions={0}, use_global_device_ids=true | all-gather | bytes 786432 | tf_op jit(solution)/shard_map/all_gather | solution.py:282
  27.6 0.1 first_terms.1
  27.6 23.6 %all_to_all.15.parts_ref = bf16[16,64,128]{2,1,0:T(8,128)(2,1)S(1)} all-to-all(bf16[16,64,128]{2,1,0:T(8,128)(2,1)S(1)} %first_terms.1), channel_id=1, replica_groups={{0,2,4,6,8,10,12,14,16,18,20,22,24,26,28,30},{32,34,36,38,40,42,44,46,4..., dimensions={0} | all-to-all | bytes 524288 | tf_op jit(solution)/shard_map/all_to_all | solution.py:284
  51.2 0.1 second_terms.1
  51.2 14.0 %all_to_all.16 = bf16[16,64,128]{2,1,0:T(8,128)(2,1)S(1)} all-to-all(bf16[16,64,128]{2,1,0:T(8,128)(2,1)S(1)} %get-tuple-element.19), channel_id=1, replica_groups={{0,2,4,6,8,10,12,14,16,18,20,22,24,26,28,30},{32,34,36,38,40,42,44,46,4..., dimensions={0} | all-to-all | bytes 524288 | tf_op jit(solution)/shard_map/all_to_all | solution.py:288
  65.2 2.2 %all-gather.1 = bf16[32,64,128]{2,1,0:T(8,128)(2,1)S(1)} all-gather(bf16[16,64,128]{2,1,0:T(8,128)(2,1)S(1)} %all_to_all.16), channel_id=3, replica_groups={{0,1},{2,3},{4,5},{6,7},{8,9},{10,11},{12,13},{14,15},{16,17},{18,19},{..., dimensions={0}, use_global_device_ids=true | all-gather | bytes 786432 | tf_op jit(solution)/shard_map/all_gather | solution.py:289
  67.4 0.8 %finish.1 = (f32[64,128]{1,0:T(8,128)}, f32[512,128]{1,0:T(8,128)}) custom-call(s32[1]{0:T(128)} %bitcast.core_ref, f32[64,128]{1,0:T(8,128)S(1)} %get-tuple-element.18.new_ref, bf16[2,16,64,128]{3,2,1,0:T(8,128)(2,1)S(1)} %bitcast.5), custom_call_target="tpu_custom_call" | custom-call | tf_op jit(solution)/shard_map/finish/pallas_call | solution.py:248
Async XLA Ops:
  2.2 18.3 %all-to-all-start = ((bf16[16,64,128]{2,1,0:T(8,128)(2,1)}), bf16[16,64,128]{2,1,0:T(8,128)(2,1)S(1)}, u32[]{:S(2)}, u32[]{:S(2)}) async-start(bf16[16,64,128]{2,1,0:T(8,128)(2,1)} %user_copies.1), calls=%async_computation | async-start | bytes 524288 | tf_op jit(solution)/shard_map/all_to_all | solution.py:273
  16.4 5.9 %collective-permute-start = (bf16[18,64,512]{2,1,0:T(8,128)(2,1)S(1)}, bf16[18,64,512]{2,1,0:T(8,128)(2,1)S(1)}, u32[]{:S(2)}, u32[]{:S(2)}) collective-permute-start(bf16[18,64,512]{2,1,0:T(8,128)(2,1)S(1)} %get-tuple-element.11.sent_ref), channel_id=1, source_target_pairs={{0,1},{1,0},{2,3},{3,2},{4,5},{5,4},{6,7},{7,6},{8,9},{9,8},{10,11... | collective-permute-start | bytes 3538952 | tf_op jit(solution)/shard_map/ppermute | solution.py:275

commit v5 on v4

v5 whole, which is shorter than its diff:
```python
import functools
import jax
import jax.numpy as jnp
from jax import lax
from jax.experimental import pallas as pl
from jax.experimental.pallas import tpu as pltpu
from jax.sharding import PartitionSpec as P

CHUNK = 16
STEP = 4
UNROLL = 4
FAR = 2

prior_shape = 0.3
f32 = jnp.float32
bf16 = jnp.bfloat16
ROWS = (((0,), (0,)), ((), ()))
LANES = (((1,), (1,)), ((), ()))


def factors(shape, rate):
    y = shape + 6.0
    u = shape * (shape + 5.0)
    below = (2.0 * shape + 5.0) * ((3.0 * u + 20.0) * u + 24.0) / (u * ((u + 10.0) * u + 24.0))
    w = 1.0 / y
    v = w * w
    tail = 0.5 * w + v * (1.0 / 12.0 - v * (1.0 / 120.0 - v * (1.0 / 252.0)))
    return (y / rate * jnp.exp(-(tail + below))).astype(bf16)


def this_core():
    return lax.axis_index("shard") & 1


def user_copies(shape_ref, rate_ref, out_ref):
    out_ref[...] = jnp.broadcast_to(factors(shape_ref[...], rate_ref[...])[None], out_ref.shape)


def add_clicks(
    slots, edge, rows_in, cols_in, count_in, clicks_ref, shape_in, rate_in, kept_ref, tail_ref, sent_ref,
    total, held, staged, rows_ref, cols_ref, count_ref, shape_ref, rate_ref, sems, more_sems,
):
    chunks = slots // CHUNK
    blocks, items = total.shape[0] - 1, total.shape[2]
    half = staged.shape[1]
    near = kept_ref.shape[0]

    def copy(c):
        part = pl.ds(c * CHUNK, CHUNK)
        return pltpu.make_async_copy(clicks_ref.at[part], held.at[part], sems.at[c])

    pairs = ((shape_in, shape_ref), (rate_in, rate_ref), (rows_in, rows_ref), (cols_in, cols_ref), (count_in, count_ref))
    more = [pltpu.make_async_copy(source, target, more_sems.at[i]) for i, (source, target) in enumerate(pairs)]
    for one in more:
        one.start()
    for c in range(chunks):
        copy(c).start()

    def clear(r, carry):
        total[r] = jnp.zeros(total.shape[1:], f32)
        return carry

    lax.fori_loop(0, blocks, clear, 0)
    for one in more[2:]:
        one.wait()
    count = count_ref[0]

    def add(i, carry):
        slots_of = [i * UNROLL + k for k in range(UNROLL)]
        rows = [jnp.where(t < count, rows_ref[t], blocks) for t in slots_of]
        cols = [pl.ds(pl.multiple_of(cols_ref[t] * edge, edge), edge) for t in slots_of]
        for t, row, part in zip(slots_of, rows, cols):
            total[row, :, part] += held[t].astype(f32)
        return carry

    for c in range(chunks):
        copy(c).wait()
        steps = jnp.clip(count - c * CHUNK, 0, CHUNK)
        lax.fori_loop(c * CHUNK // UNROLL, (c * CHUNK + steps + UNROLL - 1) // UNROLL, add, 0)

    first = this_core() * half
    kept = pl.ds(pl.multiple_of(first, half), half)
    sent = pl.ds(pl.multiple_of(half - first, half), half)

    def keep_tail(r, carry):
        staged[r] = total[near + r, kept, :].astype(bf16)
        return carry

    lax.fori_loop(0, blocks - near, keep_tail, 0)
    out = pltpu.make_async_copy(staged, tail_ref, sems.at[chunks])
    out.start()
    more[0].wait()
    more[1].wait()
    wide = items // edge
    parts = items // half
    each = blocks // parts
    for j in range(parts):
        part = slice(j * half, (j + 1) * half)
        lanes = slice(j % wide * edge, (j % wide + 1) * edge)
        sent_ref[blocks + j // wide, :, lanes] = factors(shape_ref[part], rate_ref[part])
        for r in range(j * each, (j + 1) * each):
            sent_ref[r] = total[r, sent, :].astype(bf16)
            if r < near:
                kept_ref[r] = total[r, kept, :].astype(bf16)
    out.wait()


def pair_clicks(tile_rows, tile_cols, tile_count, clicks, item_shape, item_rate, blocks):
    slots, edge, _ = clicks.shape
    items, comps = item_shape.shape
    half = edge // 2
    vmem, hbm = pl.BlockSpec(memory_space=pltpu.VMEM), pl.BlockSpec(memory_space=pltpu.HBM)
    return pl.pallas_call(
        functools.partial(add_clicks, slots, edge),
        out_shape=(
            pltpu.VMEM((blocks - FAR, half, items), bf16),
            pltpu.HBM((FAR, half, items), bf16),
            pltpu.VMEM((blocks + comps // half, half, items), bf16),
        ),
        in_specs=[hbm] * 6,
        out_specs=(vmem, hbm, vmem),
        scratch_shapes=[
            pltpu.VMEM((blocks + 1, edge, items), f32),
            pltpu.VMEM((slots, edge, edge), bf16),
            pltpu.VMEM((FAR, half, items), bf16),
            pltpu.SMEM(tile_rows.shape, jnp.int32),
            pltpu.SMEM(tile_cols.shape, jnp.int32),
            pltpu.SMEM(tile_count.shape, jnp.int32),
            pltpu.VMEM(item_shape.shape, f32),
            pltpu.VMEM(item_rate.shape, f32),
            pltpu.SemaphoreType.DMA((slots // CHUNK + 1,)),
            pltpu.SemaphoreType.DMA((5,)),
        ],
        compiler_params=pltpu.CompilerParams(vmem_limit_bytes=56 << 20),
        cost_estimate=pl.CostEstimate(flops=slots * edge * edge, bytes_accessed=2 * slots * edge * edge, transcendentals=0),
        name="pair_clicks",
    )(tile_rows, tile_cols, tile_count, clicks, item_shape, item_rate)


def sent_factors(sent_ref, blocks, comps):
    return jnp.concatenate(
        [sent_ref[q, :, j : j + comps] for q in range(blocks, sent_ref.shape[0]) for j in range(0, sent_ref.shape[2], comps)],
        0,
    )


def add_terms(a_ref, counts_of, b, add_users, total):
    blocks, half, comps = a_ref.shape
    rows = STEP * half
    total[...] = jnp.zeros_like(total)
    for i in range(blocks // STEP):
        at = pl.ds(i * STEP, STEP)
        a = a_ref[at].reshape(rows, comps)
        denom = lax.dot_general(a, b, LANES, preferred_element_type=f32)
        ratio = (counts_of(i).reshape(rows, -1).astype(f32) / denom).astype(bf16)
        product = jnp.dot(ratio, b, preferred_element_type=f32)
        add_users(at, (a.astype(f32) * product).reshape(STEP, half, comps))
        total[...] += lax.dot_general(a, ratio, ROWS, preferred_element_type=f32)


def place_items(b, sums, out_ref, part, items_of):
    blocks = out_ref.shape[0]
    terms = (b.astype(f32) * sums.T).reshape(blocks, items_of, -1)
    out_ref[:, pl.ds(pl.multiple_of(part * items_of, items_of), items_of), :] = terms


def own_items(a_ref, sent_ref, kept_ref, tail_ref, user_ref, item_ref, same_ref, total, held, sem):
    blocks, _, comps = a_ref.shape
    copy = pltpu.make_async_copy(tail_ref, held, sem)
    copy.start()
    b = sent_factors(sent_ref, blocks, comps)

    def counts_of(i):
        if i == blocks // STEP - 2:
            copy.wait()
        if (i + 1) * STEP <= kept_ref.shape[0]:
            return kept_ref[i * STEP : (i + 1) * STEP]
        return jnp.concatenate([kept_ref[i * STEP :], held[...]], 0)

    def add_users(at, terms):
        user_ref[at] = terms

    add_terms(a_ref, counts_of, b, add_users, total)
    place_items(b, total[...], item_ref, this_core(), b.shape[0] // blocks)


def near_items(a, sent, kept, tail):
    vmem, hbm = pl.BlockSpec(memory_space=pltpu.VMEM), pl.BlockSpec(memory_space=pltpu.HBM)
    items = sent.shape[2]
    users, item_sums, _ = pl.pallas_call(
        own_items,
        out_shape=(pltpu.VMEM(a.shape, f32), pltpu.VMEM(a.shape, f32), pltpu.HBM(tail.shape, bf16)),
        in_specs=[vmem, vmem, vmem, hbm],
        out_specs=(vmem, vmem, hbm),
        scratch_shapes=[pltpu.VMEM((a.shape[2], items), f32), pltpu.VMEM(tail.shape, bf16), pltpu.SemaphoreType.DMA],
        input_output_aliases={3: 2},
        compiler_params=pltpu.CompilerParams(vmem_limit_bytes=24 << 20),
        cost_estimate=pl.CostEstimate(flops=1 << 34, bytes_accessed=1 << 24, transcendentals=0),
        name="own_items",
    )(a, sent, kept, tail)
    return users, item_sums


def other_items(a_ref, got_ref, user_ref, item_ref, keep_ref, send_ref, total, users, items):
    core = this_core()
    blocks, half, comps = a_ref.shape
    b = sent_factors(got_ref, blocks, comps)

    def counts_of(i):
        return got_ref[i * STEP : (i + 1) * STEP]

    def add_users(at, terms):
        users[at] = user_ref[at] + terms

    add_terms(a_ref, counts_of, b, add_users, total)
    rows = b.shape[0] // blocks
    items[...] = item_ref[...]
    place_items(b, total[...], items, 1 - core, rows)

    @pl.when(core == 0)
    def _():
        keep_ref[...] = users[...]
        send_ref[...] = items[...].astype(bf16)

    @pl.when(core != 0)
    def _():
        keep_ref[...] = items[...]
        send_ref[...] = users[...].astype(bf16)


def first_terms(keep_ref, sent_ref, out_ref):
    other = jnp.where(this_core() == 0, 0.0, sent_ref[0].astype(f32))
    out_ref[...] = (keep_ref[...] + other).astype(bf16)


def second_terms(parts_ref, sent_ref, new_ref, out_ref):
    total = jnp.sum(parts_ref[...].astype(f32), 0)
    new_ref[...] = prior_shape + total

    @pl.when(this_core() == 0)
    def _():
        out_ref[...] = sent_ref[1]

    @pl.when(this_core() != 0)
    def _():
        out_ref[...] = jnp.broadcast_to(total.astype(bf16)[None], out_ref.shape)


def finish(new_ref, parts_ref, user_ref, item_ref):
    rows = parts_ref.shape[2] // 2

    @pl.when(this_core() == 0)
    def _():
        user_ref[...] = new_ref[...]
        item_ref[...] = prior_shape + parts_ref[1, :, :rows].astype(f32).reshape(item_ref.shape)

    @pl.when(this_core() != 0)
    def _():
        user_ref[...] = prior_shape + jnp.sum(parts_ref[0].astype(f32), 0)
        item_ref[...] = prior_shape + parts_ref[1, :, rows:].astype(f32).reshape(item_ref.shape)


def small(kernel, out_shape, *operands, scratch=(), limit=24):
    vmem = pl.BlockSpec(memory_space=pltpu.VMEM)
    return pl.pallas_call(
        kernel,
        out_shape=out_shape,
        in_specs=[vmem] * len(operands),
        out_specs=jax.tree.map(lambda _: vmem, out_shape),
        scratch_shapes=list(scratch),
        compiler_params=pltpu.CompilerParams(vmem_limit_bytes=limit << 20),
        name=kernel.__name__,
    )(*operands)


def body(n_group, n_shard, user_shape, user_rate, item_shape, item_rate, tile_rows, tile_cols, clicks, tile_count):
    own, comps = user_shape.shape
    items = item_shape.shape[0]
    edge = clicks.shape[1]
    chips = n_shard // 2
    both = ("group", "shard")
    swap = [(s, s ^ 1) for s in range(n_shard)]
    pairs = [[2 * r, 2 * r + 1] for r in range(chips)]
    same_core = [[2 * r + c for r in range(chips)] for c in range(2)]
    users_or_items = [[g * n_shard + 2 * r for r in range(chips)] for g in range(n_group)]
    users_or_items += [[g * n_shard + 2 * r + 1 for g in range(n_group)] for r in range(chips)]

    copies = small(user_copies, jax.ShapeDtypeStruct((chips, own, comps), bf16), user_shape, user_rate, limit=56)
    a_mine = lax.all_to_all(copies, "shard", 0, 0, axis_index_groups=same_core)
    kept, tail, sent = pair_clicks(tile_rows, tile_cols, tile_count, clicks, item_shape, item_rate, chips)
    other = lax.ppermute(sent, "shard", swap)
    whole = (chips, own, comps)
    users, item_sums = near_items(a_mine, sent, kept, tail)
    keep, send = small(
        other_items, (pltpu.VMEM(whole, f32), pltpu.VMEM(whole, bf16)), a_mine, other, users, item_sums,
        scratch=(pltpu.VMEM((comps, items), f32), pltpu.VMEM(whole, f32), pltpu.VMEM(whole, f32)),
    )
    sent = lax.all_gather(send, "shard", axis_index_groups=pairs)
    terms = small(first_terms, jax.ShapeDtypeStruct(whole, bf16), keep, sent)
    parts = lax.all_to_all(terms, both, 0, 0, axis_index_groups=users_or_items)
    new, terms = small(
        second_terms, (jax.ShapeDtypeStruct((own, comps), f32), jax.ShapeDtypeStruct(whole, bf16)), parts, sent
    )
    parts = lax.all_to_all(terms, both, 0, 0, axis_index_groups=users_or_items)
    parts = lax.all_gather(parts, "shard", axis_index_groups=pairs)
    return small(
        finish, (jax.ShapeDtypeStruct((own, comps), f32), jax.ShapeDtypeStruct((items, comps), f32)), new, parts
    )


def solution(mesh):
    return jax.shard_map(
        functools.partial(body, mesh.shape["group"], mesh.shape["shard"]),
        mesh=mesh,
        in_specs=(
            P(("group", "shard"), None),
            P(("group", "shard"), None),
            P("shard", None),
            P("shard", None),
            P(("group", "shard")),
            P(("group", "shard")),
            P(("group", "shard"), None, None),
            P(("group", "shard")),
        ),
        out_specs=(P(("group", "shard"), None), P("shard", None)),
        check_vma=False,
    )
```

time: 68.6 us -> 68.3 us (level)
  waiting for transfers between devices: 0.86 us -> 2.09 us
  starting transfers between devices: 13 us -> 12.2 us
  Pallas kernels: 9.39 us -> 8.66 us
    all_to_all x1, waiting for transfers between devices: 0.62 us -> 2.09 us  [body(): a_mine = lax.all_to_all(copies, 'shard', 0, 0, axis_index_groups=same_core)]
    ppermute x1, starting transfers between devices: 3.42 us -> 2.63 us  [body(): other = lax.ppermute(sent, 'shard', swap)]
  transfers between devices with their start and end apart: 2 -> 2, of which waited for: 2 -> 1; matrix products, arithmetic and copies ran while one was open for 0% -> 0% of each run, Pallas kernels for 8% -> 7%
where the time goes in v5:
time: 68.3 us; the launch traced here: 67.9 us
  blocking collectives  43.6 us (64%)
  starting transfers between devices  12.2 us (18%)
  Pallas kernels  8.66 us (13%)
  waiting for transfers between devices  2.09 us (3%)
  between operations  1.34 us (2%)
    all_to_all x2, blocking collectives, body(): parts = lax.all_to_all(terms, both, 0, 0, axis_index_groups=users_or_items)  37.3 us
    all_to_all x1, starting transfers between devices, body(): a_mine = lax.all_to_all(copies, 'shard', 0, 0, axis_index_groups=same_core)  9.56 us
    all_gather x1, blocking collectives, body(): sent = lax.all_gather(send, 'shard', axis_index_groups=pairs)  4.13 us
    pallas_call x5, Pallas kernels, small(): pl.pallas_call(kernel, out_shape=out_shape, in_specs=[vmem] * len(operand...  3.79 us
    pallas_call x1, Pallas kernels, pair_clicks(): pl.pallas_call(functools.partial(add_clicks, slots, edge), out_shape=(plt...  3.35 us
    ppermute x1, starting transfers between devices, body(): other = lax.ppermute(sent, 'shard', swap)  2.63 us
    all_gather x1, blocking collectives, body(): parts = lax.all_gather(parts, 'shard', axis_index_groups=pairs)  2.17 us
    all_to_all x1, waiting for transfers between devices, body(): a_mine = lax.all_to_all(copies, 'shard', 0, 0, axis_index_groups=same_core)  2.09 us
  transfers between devices with their start and end apart: 2, of which 1 were waited for; matrix products, arithmetic and copies ran while one was open for 0% of the time, Pallas kernels for 7%

profile of v5, /device:TPU:1, one launch (start us, length us, event | category | flops | bytes accessed | tf_op | source)
XLA Modules:
  0.0 67.9 jit_solution(6867368988450231797)
XLA Ops:
  0.6 1.5 %user_copies.1 = bf16[16,64,128]{2,1,0:T(8,128)(2,1)} custom-call(f32[64,128]{1,0:T(8,128)} %shape_ref.1, f32[64,128]{1,0:T(8,128)} %rate_ref.1), custom_call_target="tpu_custom_call" | custom-call | tf_op jit(solution)/shard_map/user_copies/pallas_call | solution.py:265
  2.2 9.6 %all-to-all-start = ((bf16[16,64,128]{2,1,0:T(8,128)(2,1)}), bf16[16,64,128]{2,1,0:T(8,128)(2,1)S(1)}, u32[]{:S(2)}, u32[]{:S(2)}) async-start(bf16[16,64,128]{2,1,0:T(8,128)(2,1)} %user_copies.1), calls=%async_computation | async-start | bytes 524288 | tf_op jit(solution)/shard_map/all_to_all | solution.py:289
  12.4 3.3 %pair_clicks.1 = (bf16[14,64,512]{2,1,0:T(8,128)(2,1)S(1)}, bf16[2,64,512]{2,1,0:T(8,128)(2,1)}, bf16[18,64,512]{2,1,0:T(8,128)(2,1)S(1)}) custom-call(s32[128]{0:T(128)} %rows_in.1, s32[128]{0:T(128)} %cols_in.1, s32[1]{0:T(128)S(6)} %copy.12.count_in, bf16[128,128,128]{2,1,0:T(8,128)(2,1)} %clicks_ref.1, f32[512,128]{1,0:T(8,128)} %shape_in.1, ...), custom_call_target="tpu_custom_call" | custom-call | flops 2097152 | bytes 4194304 | tf_op jit(solution)/shard_map/pair_clicks/pallas_call | solution.py:113
  15.7 2.6 %collective-permute-start = (bf16[18,64,512]{2,1,0:T(8,128)(2,1)S(1)}, bf16[18,64,512]{2,1,0:T(8,128)(2,1)S(1)}, u32[]{:S(2)}, u32[]{:S(2)}) collective-permute-start(bf16[18,64,512]{2,1,0:T(8,128)(2,1)S(1)} %get-tuple-element.11.sent_ref), channel_id=1, source_target_pairs={{0,1},{1,0},{2,3},{3,2},{4,5},{5,4},{6,7},{7,6},{8,9},{9,8},{10,11... | collective-permute-start | bytes 3538952 | tf_op jit(solution)/shard_map/ppermute | solution.py:291
  18.4 2.1 %all-to-all-done.a_ref = bf16[16,64,128]{2,1,0:T(8,128)(2,1)S(1)} async-done(((bf16[16,64,128]{2,1,0:T(8,128)(2,1)}), bf16[16,64,128]{2,1,0:T(8,128)(2,1)S(1)}, u32[]{:S(2)}, u32[]{:S(2)}) %all-to-all-start) | async-done | bytes 262176 | tf_op jit(solution)/shard_map/all_to_all | solution.py:289
  20.5 1.5 %own_items.1 = (f32[16,64,128]{2,1,0:T(8,128)S(1)}, f32[16,64,128]{2,1,0:T(8,128)S(1)}, bf16[2,64,512]{2,1,0:T(8,128)(2,1)}) custom-call(bf16[16,64,128]{2,1,0:T(8,128)(2,1)S(1)} %all-to-all-done.a_ref, bf16[18,64,512]{2,1,0:T(8,128)(2,1)S(1)} %get-tuple-element.11.sent_ref, ...), custom_call_target="tpu_custom_call", output_to_operand_aliasing={{2}: (3, {})} | custom-call | flops 17179869184 | bytes 16777216 | tf_op jit(solution)/shard_map/own_items/pallas_call | solution.py:190
  22.0 0.0 collective-permute-done.got_ref
  22.0 1.3 %other_items.1 = (f32[16,64,128]{2,1,0:T(8,128)S(1)}, bf16[16,64,128]{2,1,0:T(8,128)(2,1)S(1)}) custom-call(bf16[16,64,128]{2,1,0:T(8,128)(2,1)S(1)} %all-to-all-done.a_ref, bf16[18,64,512]{2,1,0:T(8,128)(2,1)S(1)} %collective-permute-done.got_ref, f32[16,64,128]{2,1,0:T(8,128)S(1)} %get-tuple-element.14.user_ref, f32[16,64,128]{2,1,0:T(8,128)S(1)} %get-tuple-element.15.item_ref), custom_call_target="tpu_custom_call" | custom-call | tf_op jit(solution)/shard_map/other_items/pallas_call | solution.py:265
  23.4 4.1 %all-gather = bf16[32,64,128]{2,1,0:T(8,128)(2,1)S(1)} all-gather(bf16[16,64,128]{2,1,0:T(8,128)(2,1)S(1)} %get-tuple-element.17), channel_id=2, replica_groups={{0,1},{2,3},{4,5},{6,7},{8,9},{10,11},{12,13},{14,15},{16,17},{18,19},{..., dimensions={0}, use_global_device_ids=true | all-gather | bytes 786432 | tf_op jit(solution)/shard_map/all_gather | solution.py:298
  27.5 0.1 first_terms.1
  27.6 23.3 %all_to_all.15.parts_ref = bf16[16,64,128]{2,1,0:T(8,128)(2,1)S(1)} all-to-all(bf16[16,64,128]{2,1,0:T(8,128)(2,1)S(1)} %first_terms.1), channel_id=1, replica_groups={{0,2,4,6,8,10,12,14,16,18,20,22,24,26,28,30},{32,34,36,38,40,42,44,46,4..., dimensions={0} | all-to-all | bytes 524288 | tf_op jit(solution)/shard_map/all_to_all | solution.py:300
  50.9 0.1 second_terms.1
  51.0 14.0 %all_to_all.16 = bf16[16,64,128]{2,1,0:T(8,128)(2,1)S(1)} all-to-all(bf16[16,64,128]{2,1,0:T(8,128)(2,1)S(1)} %get-tuple-element.19), channel_id=1, replica_groups={{0,2,4,6,8,10,12,14,16,18,20,22,24,26,28,30},{32,34,36,38,40,42,44,46,4..., dimensions={0} | all-to-all | bytes 524288 | tf_op jit(solution)/shard_map/all_to_all | solution.py:304
  65.0 2.2 %all-gather.1 = bf16[32,64,128]{2,1,0:T(8,128)(2,1)S(1)} all-gather(bf16[16,64,128]{2,1,0:T(8,128)(2,1)S(1)} %all_to_all.16), channel_id=3, replica_groups={{0,1},{2,3},{4,5},{6,7},{8,9},{10,11},{12,13},{14,15},{16,17},{18,19},{..., dimensions={0}, use_global_device_ids=true | all-gather | bytes 786432 | tf_op jit(solution)/shard_map/all_gather | solution.py:305
  67.2 0.8 %finish.1 = (f32[64,128]{1,0:T(8,128)}, f32[512,128]{1,0:T(8,128)}) custom-call(f32[64,128]{1,0:T(8,128)S(1)} %get-tuple-element.18.new_ref, bf16[2,16,64,128]{3,2,1,0:T(8,128)(2,1)S(1)} %bitcast.4), custom_call_target="tpu_custom_call" | custom-call | tf_op jit(solution)/shard_map/finish/pallas_call | solution.py:265
Async XLA Ops:
  2.2 18.3 %all-to-all-start = ((bf16[16,64,128]{2,1,0:T(8,128)(2,1)}), bf16[16,64,128]{2,1,0:T(8,128)(2,1)S(1)}, u32[]{:S(2)}, u32[]{:S(2)}) async-start(bf16[16,64,128]{2,1,0:T(8,128)(2,1)} %user_copies.1), calls=%async_computation | async-start | bytes 524288 | tf_op jit(solution)/shard_map/all_to_all | solution.py:289
  15.7 6.3 %collective-permute-start = (bf16[18,64,512]{2,1,0:T(8,128)(2,1)S(1)}, bf16[18,64,512]{2,1,0:T(8,128)(2,1)S(1)}, u32[]{:S(2)}, u32[]{:S(2)}) collective-permute-start(bf16[18,64,512]{2,1,0:T(8,128)(2,1)S(1)} %get-tuple-element.11.sent_ref), channel_id=1, source_target_pairs={{0,1},{1,0},{2,3},{3,2},{4,5},{5,4},{6,7},{7,6},{8,9},{9,8},{10,11... | collective-permute-start | bytes 3538952 | tf_op jit(solution)/shard_map/ppermute | solution.py:291

commit v6 on v5

--- a/solution.py
+++ b/solution.py
@@ -7,7 +7,6 @@
 from jax.sharding import PartitionSpec as P
 
 CHUNK = 16
-STEP = 4
 UNROLL = 4
 FAR = 2
 
@@ -144,17 +143,17 @@
     )
 
 
-def add_terms(a_ref, counts_of, b, add_users, total):
-    blocks, half, comps = a_ref.shape
-    rows = STEP * half
+def add_terms(a_ref, cuts, counts_of, b, add_users, total):
+    _, half, comps = a_ref.shape
     total[...] = jnp.zeros_like(total)
-    for i in range(blocks // STEP):
-        at = pl.ds(i * STEP, STEP)
+    for first, last in zip(cuts, cuts[1:]):
+        at = pl.ds(first, last - first)
+        rows = (last - first) * half
         a = a_ref[at].reshape(rows, comps)
         denom = lax.dot_general(a, b, LANES, preferred_element_type=f32)
-        ratio = (counts_of(i).reshape(rows, -1).astype(f32) / denom).astype(bf16)
+        ratio = (counts_of(first, last).reshape(rows, -1).astype(f32) / denom).astype(bf16)
         product = jnp.dot(ratio, b, preferred_element_type=f32)
-        add_users(at, (a.astype(f32) * product).reshape(STEP, half, comps))
+        add_users(at, (a.astype(f32) * product).reshape(-1, half, comps))
         total[...] += lax.dot_general(a, ratio, ROWS, preferred_element_type=f32)
 
 
@@ -170,17 +169,18 @@
     copy.start()
     b = sent_factors(sent_ref, blocks, comps)
 
-    def counts_of(i):
-        if i == blocks // STEP - 2:
-            copy.wait()
-        if (i + 1) * STEP <= kept_ref.shape[0]:
-            return kept_ref[i * STEP : (i + 1) * STEP]
-        return jnp.concatenate([kept_ref[i * STEP :], held[...]], 0)
+    near = kept_ref.shape[0]
+
+    def counts_of(first, last):
+        if last <= near:
+            return kept_ref[first:last]
+        copy.wait()
+        return held[...]
 
     def add_users(at, terms):
         user_ref[at] = terms
 
-    add_terms(a_ref, counts_of, b, add_users, total)
+    add_terms(a_ref, (0, near // 2, near, blocks), counts_of, b, add_users, total)
     place_items(b, total[...], item_ref, this_core(), b.shape[0] // blocks)
 
 
@@ -206,13 +206,13 @@
     blocks, half, comps = a_ref.shape
     b = sent_factors(got_ref, blocks, comps)
 
-    def counts_of(i):
-        return got_ref[i * STEP : (i + 1) * STEP]
+    def counts_of(first, last):
+        return got_ref[first:last]
 
     def add_users(at, terms):
         users[at] = user_ref[at] + terms
 
-    add_terms(a_ref, counts_of, b, add_users, total)
+    add_terms(a_ref, (0, blocks // 2, blocks), counts_of, b, add_users, total)
     rows = b.shape[0] // blocks
     items[...] = item_ref[...]
     place_items(b, total[...], items, 1 - core, rows)

time: 68.3 us -> 68.3 us (level)
  no operation moved by 1% of the time
where the time goes in v6:
time: 68.3 us; the launch traced here: 68 us
  blocking collectives  43.9 us (64%)
  starting transfers between devices  12.4 us (18%)
  Pallas kernels  8.21 us (12%)
  waiting for transfers between devices  2.11 us (3%)
  between operations  1.34 us (2%)
    all_to_all x2, blocking collectives, body(): parts = lax.all_to_all(terms, both, 0, 0, axis_index_groups=users_or_items)  37.6 us
    all_to_all x1, starting transfers between devices, body(): a_mine = lax.all_to_all(copies, 'shard', 0, 0, axis_index_groups=same_core)  9.56 us
    all_gather x1, blocking collectives, body(): sent = lax.all_gather(send, 'shard', axis_index_groups=pairs)  4.13 us
    pallas_call x5, Pallas kernels, small(): pl.pallas_call(kernel, out_shape=out_shape, in_specs=[vmem] * len(operand...  3.71 us
    pallas_call x1, Pallas kernels, pair_clicks(): pl.pallas_call(functools.partial(add_clicks, slots, edge), out_shape=(plt...  3.11 us
    ppermute x1, starting transfers between devices, body(): other = lax.ppermute(sent, 'shard', swap)  2.84 us
    all_gather x1, blocking collectives, body(): parts = lax.all_gather(parts, 'shard', axis_index_groups=pairs)  2.17 us
    all_to_all x1, waiting for transfers between devices, body(): a_mine = lax.all_to_all(copies, 'shard', 0, 0, axis_index_groups=same_core)  2.11 us
  transfers between devices with their start and end apart: 2, of which 1 were waited for; matrix products, arithmetic and copies ran while one was open for 0% of the time, Pallas kernels for 7%

profile of v6, /device:TPU:1, one launch (start us, length us, event | category | flops | bytes accessed | tf_op | source)
XLA Modules:
  0.0 68.0 jit_solution(17078405648685961953)
XLA Ops:
  0.6 1.5 %user_copies.1 = bf16[16,64,128]{2,1,0:T(8,128)(2,1)} custom-call(f32[64,128]{1,0:T(8,128)} %shape_ref.1, f32[64,128]{1,0:T(8,128)} %rate_ref.1), custom_call_target="tpu_custom_call" | custom-call | tf_op jit(solution)/shard_map/user_copies/pallas_call | solution.py:265
  2.2 9.6 %all-to-all-start = ((bf16[16,64,128]{2,1,0:T(8,128)(2,1)}), bf16[16,64,128]{2,1,0:T(8,128)(2,1)S(1)}, u32[]{:S(2)}, u32[]{:S(2)}) async-start(bf16[16,64,128]{2,1,0:T(8,128)(2,1)} %user_copies.1), calls=%async_computation | async-start | bytes 524288 | tf_op jit(solution)/shard_map/all_to_all | solution.py:289
  12.4 3.1 %pair_clicks.1 = (bf16[14,64,512]{2,1,0:T(8,128)(2,1)S(1)}, bf16[2,64,512]{2,1,0:T(8,128)(2,1)}, bf16[18,64,512]{2,1,0:T(8,128)(2,1)S(1)}) custom-call(s32[128]{0:T(128)} %rows_in.1, s32[128]{0:T(128)} %cols_in.1, s32[1]{0:T(128)S(6)} %copy.12.count_in, bf16[128,128,128]{2,1,0:T(8,128)(2,1)} %clicks_ref.1, f32[512,128]{1,0:T(8,128)} %shape_in.1, ...), custom_call_target="tpu_custom_call" | custom-call | flops 2097152 | bytes 4194304 | tf_op jit(solution)/shard_map/pair_clicks/pallas_call | solution.py:112
  15.5 2.8 %collective-permute-start = (bf16[18,64,512]{2,1,0:T(8,128)(2,1)S(1)}, bf16[18,64,512]{2,1,0:T(8,128)(2,1)S(1)}, u32[]{:S(2)}, u32[]{:S(2)}) collective-permute-start(bf16[18,64,512]{2,1,0:T(8,128)(2,1)S(1)} %get-tuple-element.11.sent_ref), channel_id=1, source_target_pairs={{0,1},{1,0},{2,3},{3,2},{4,5},{5,4},{6,7},{7,6},{8,9},{9,8},{10,11... | collective-permute-start | bytes 3538952 | tf_op jit(solution)/shard_map/ppermute | solution.py:291
  18.4 2.1 %all-to-all-done.a_ref = bf16[16,64,128]{2,1,0:T(8,128)(2,1)S(1)} async-done(((bf16[16,64,128]{2,1,0:T(8,128)(2,1)}), bf16[16,64,128]{2,1,0:T(8,128)(2,1)S(1)}, u32[]{:S(2)}, u32[]{:S(2)}) %all-to-all-start) | async-done | bytes 262176 | tf_op jit(solution)/shard_map/all_to_all | solution.py:289
  20.5 1.4 %own_items.1 = (f32[16,64,128]{2,1,0:T(8,128)S(1)}, f32[16,64,128]{2,1,0:T(8,128)S(1)}, bf16[2,64,512]{2,1,0:T(8,128)(2,1)}) custom-call(bf16[16,64,128]{2,1,0:T(8,128)(2,1)S(1)} %all-to-all-done.a_ref, bf16[18,64,512]{2,1,0:T(8,128)(2,1)S(1)} %get-tuple-element.11.sent_ref, ...), custom_call_target="tpu_custom_call", output_to_operand_aliasing={{2}: (3, {})} | custom-call | flops 17179869184 | bytes 16777216 | tf_op jit(solution)/shard_map/own_items/pallas_call | solution.py:190
  21.9 0.0 collective-permute-done.got_ref
  21.9 1.3 %other_items.1 = (f32[16,64,128]{2,1,0:T(8,128)S(1)}, bf16[16,64,128]{2,1,0:T(8,128)(2,1)S(1)}) custom-call(bf16[16,64,128]{2,1,0:T(8,128)(2,1)S(1)} %all-to-all-done.a_ref, bf16[18,64,512]{2,1,0:T(8,128)(2,1)S(1)} %collective-permute-done.got_ref, f32[16,64,128]{2,1,0:T(8,128)S(1)} %get-tuple-element.14.user_ref, f32[16,64,128]{2,1,0:T(8,128)S(1)} %get-tuple-element.15.item_ref), custom_call_target="tpu_custom_call" | custom-call | tf_op jit(solution)/shard_map/other_items/pallas_call | solution.py:265
  23.2 4.1 %all-gather = bf16[32,64,128]{2,1,0:T(8,128)(2,1)S(1)} all-gather(bf16[16,64,128]{2,1,0:T(8,128)(2,1)S(1)} %get-tuple-element.17), channel_id=2, replica_groups={{0,1},{2,3},{4,5},{6,7},{8,9},{10,11},{12,13},{14,15},{16,17},{18,19},{..., dimensions={0}, use_global_device_ids=true | all-gather | bytes 786432 | tf_op jit(solution)/shard_map/all_gather | solution.py:298
  27.3 0.1 first_terms.1
  27.4 23.5 %all_to_all.15.parts_ref = bf16[16,64,128]{2,1,0:T(8,128)(2,1)S(1)} all-to-all(bf16[16,64,128]{2,1,0:T(8,128)(2,1)S(1)} %first_terms.1), channel_id=1, replica_groups={{0,2,4,6,8,10,12,14,16,18,20,22,24,26,28,30},{32,34,36,38,40,42,44,46,4..., dimensions={0} | all-to-all | bytes 524288 | tf_op jit(solution)/shard_map/all_to_all | solution.py:300
  50.8 0.1 second_terms.1
  50.9 14.2 %all_to_all.16 = bf16[16,64,128]{2,1,0:T(8,128)(2,1)S(1)} all-to-all(bf16[16,64,128]{2,1,0:T(8,128)(2,1)S(1)} %get-tuple-element.19), channel_id=1, replica_groups={{0,2,4,6,8,10,12,14,16,18,20,22,24,26,28,30},{32,34,36,38,40,42,44,46,4..., dimensions={0} | all-to-all | bytes 524288 | tf_op jit(solution)/shard_map/all_to_all | solution.py:304
  65.1 2.2 %all-gather.1 = bf16[32,64,128]{2,1,0:T(8,128)(2,1)S(1)} all-gather(bf16[16,64,128]{2,1,0:T(8,128)(2,1)S(1)} %all_to_all.16), channel_id=3, replica_groups={{0,1},{2,3},{4,5},{6,7},{8,9},{10,11},{12,13},{14,15},{16,17},{18,19},{..., dimensions={0}, use_global_device_ids=true | all-gather | bytes 786432 | tf_op jit(solution)/shard_map/all_gather | solution.py:305
  67.2 0.8 %finish.1 = (f32[64,128]{1,0:T(8,128)}, f32[512,128]{1,0:T(8,128)}) custom-call(f32[64,128]{1,0:T(8,128)S(1)} %get-tuple-element.18.new_ref, bf16[2,16,64,128]{3,2,1,0:T(8,128)(2,1)S(1)} %bitcast.4), custom_call_target="tpu_custom_call" | custom-call | tf_op jit(solution)/shard_map/finish/pallas_call | solution.py:265
Async XLA Ops:
  2.2 18.3 %all-to-all-start = ((bf16[16,64,128]{2,1,0:T(8,128)(2,1)}), bf16[16,64,128]{2,1,0:T(8,128)(2,1)S(1)}, u32[]{:S(2)}, u32[]{:S(2)}) async-start(bf16[16,64,128]{2,1,0:T(8,128)(2,1)} %user_copies.1), calls=%async_computation | async-start | bytes 524288 | tf_op jit(solution)/shard_map/all_to_all | solution.py:289
  15.5 6.4 %collective-permute-start = (bf16[18,64,512]{2,1,0:T(8,128)(2,1)S(1)}, bf16[18,64,512]{2,1,0:T(8,128)(2,1)S(1)}, u32[]{:S(2)}, u32[]{:S(2)}) collective-permute-start(bf16[18,64,512]{2,1,0:T(8,128)(2,1)S(1)} %get-tuple-element.11.sent_ref), channel_id=1, source_target_pairs={{0,1},{1,0},{2,3},{3,2},{4,5},{5,4},{6,7},{7,6},{8,9},{9,8},{10,11... | collective-permute-start | bytes 3538952 | tf_op jit(solution)/shard_map/ppermute | solution.py:291

commit v7 on v6

--- a/solution.py
+++ b/solution.py
@@ -7,7 +7,7 @@
 from jax.sharding import PartitionSpec as P
 
 CHUNK = 16
-UNROLL = 4
+UNROLL = 8
 FAR = 2
 
 prior_shape = 0.3

time: 68.3 us -> 68.1 us (level)
  no operation moved by 1% of the time
where the time goes in v7:
time: 68.1 us; the launch traced here: 67.7 us
  blocking collectives  43.7 us (64%)
  starting transfers between devices  12.4 us (18%)
  Pallas kernels  8.19 us (12%)
  waiting for transfers between devices  2.11 us (3%)
  between operations  1.34 us (2%)
    all_to_all x2, blocking collectives, body(): parts = lax.all_to_all(terms, both, 0, 0, axis_index_groups=users_or_items)  37.4 us
    all_to_all x1, starting transfers between devices, body(): a_mine = lax.all_to_all(copies, 'shard', 0, 0, axis_index_groups=same_core)  9.56 us
    all_gather x1, blocking collectives, body(): sent = lax.all_gather(send, 'shard', axis_index_groups=pairs)  4.13 us
    pallas_call x5, Pallas kernels, small(): pl.pallas_call(kernel, out_shape=out_shape, in_specs=[vmem] * len(operand...  3.71 us
    pallas_call x1, Pallas kernels, pair_clicks(): pl.pallas_call(functools.partial(add_clicks, slots, edge), out_shape=(plt...  3.09 us
    ppermute x1, starting transfers between devices, body(): other = lax.ppermute(sent, 'shard', swap)  2.86 us
    all_gather x1, blocking collectives, body(): parts = lax.all_gather(parts, 'shard', axis_index_groups=pairs)  2.17 us
    all_to_all x1, waiting for transfers between devices, body(): a_mine = lax.all_to_all(copies, 'shard', 0, 0, axis_index_groups=same_core)  2.11 us
  transfers between devices with their start and end apart: 2, of which 1 were waited for; matrix products, arithmetic and copies ran while one was open for 0% of the time, Pallas kernels for 7%

profile of v7, /device:TPU:1, one launch (start us, length us, event | category | flops | bytes accessed | tf_op | source)
XLA Modules:
  0.0 67.7 jit_solution(17510752608601136944)
XLA Ops:
  0.6 1.5 %user_copies.1 = bf16[16,64,128]{2,1,0:T(8,128)(2,1)} custom-call(f32[64,128]{1,0:T(8,128)} %shape_ref.1, f32[64,128]{1,0:T(8,128)} %rate_ref.1), custom_call_target="tpu_custom_call" | custom-call | tf_op jit(solution)/shard_map/user_copies/pallas_call | solution.py:265
  2.2 9.6 %all-to-all-start = ((bf16[16,64,128]{2,1,0:T(8,128)(2,1)}), bf16[16,64,128]{2,1,0:T(8,128)(2,1)S(1)}, u32[]{:S(2)}, u32[]{:S(2)}) async-start(bf16[16,64,128]{2,1,0:T(8,128)(2,1)} %user_copies.1), calls=%async_computation | async-start | bytes 524288 | tf_op jit(solution)/shard_map/all_to_all | solution.py:289
  12.4 3.1 %pair_clicks.1 = (bf16[14,64,512]{2,1,0:T(8,128)(2,1)S(1)}, bf16[2,64,512]{2,1,0:T(8,128)(2,1)}, bf16[18,64,512]{2,1,0:T(8,128)(2,1)S(1)}) custom-call(s32[128]{0:T(128)} %rows_in.1, s32[128]{0:T(128)} %cols_in.1, s32[1]{0:T(128)S(6)} %copy.12.count_in, bf16[128,128,128]{2,1,0:T(8,128)(2,1)} %clicks_ref.1, f32[512,128]{1,0:T(8,128)} %shape_in.1, ...), custom_call_target="tpu_custom_call" | custom-call | flops 2097152 | bytes 4194304 | tf_op jit(solution)/shard_map/pair_clicks/pallas_call | solution.py:112
  15.5 2.9 %collective-permute-start = (bf16[18,64,512]{2,1,0:T(8,128)(2,1)S(1)}, bf16[18,64,512]{2,1,0:T(8,128)(2,1)S(1)}, u32[]{:S(2)}, u32[]{:S(2)}) collective-permute-start(bf16[18,64,512]{2,1,0:T(8,128)(2,1)S(1)} %get-tuple-element.11.sent_ref), channel_id=1, source_target_pairs={{0,1},{1,0},{2,3},{3,2},{4,5},{5,4},{6,7},{7,6},{8,9},{9,8},{10,11... | collective-permute-start | bytes 3538952 | tf_op jit(solution)/shard_map/ppermute | solution.py:291
  18.4 2.1 %all-to-all-done.a_ref = bf16[16,64,128]{2,1,0:T(8,128)(2,1)S(1)} async-done(((bf16[16,64,128]{2,1,0:T(8,128)(2,1)}), bf16[16,64,128]{2,1,0:T(8,128)(2,1)S(1)}, u32[]{:S(2)}, u32[]{:S(2)}) %all-to-all-start) | async-done | bytes 262176 | tf_op jit(solution)/shard_map/all_to_all | solution.py:289
  20.5 1.4 %own_items.1 = (f32[16,64,128]{2,1,0:T(8,128)S(1)}, f32[16,64,128]{2,1,0:T(8,128)S(1)}, bf16[2,64,512]{2,1,0:T(8,128)(2,1)}) custom-call(bf16[16,64,128]{2,1,0:T(8,128)(2,1)S(1)} %all-to-all-done.a_ref, bf16[18,64,512]{2,1,0:T(8,128)(2,1)S(1)} %get-tuple-element.11.sent_ref, ...), custom_call_target="tpu_custom_call", output_to_operand_aliasing={{2}: (3, {})} | custom-call | flops 17179869184 | bytes 16777216 | tf_op jit(solution)/shard_map/own_items/pallas_call | solution.py:190
  21.9 0.0 collective-permute-done.got_ref
  21.9 1.3 %other_items.1 = (f32[16,64,128]{2,1,0:T(8,128)S(1)}, bf16[16,64,128]{2,1,0:T(8,128)(2,1)S(1)}) custom-call(bf16[16,64,128]{2,1,0:T(8,128)(2,1)S(1)} %all-to-all-done.a_ref, bf16[18,64,512]{2,1,0:T(8,128)(2,1)S(1)} %collective-permute-done.got_ref, f32[16,64,128]{2,1,0:T(8,128)S(1)} %get-tuple-element.14.user_ref, f32[16,64,128]{2,1,0:T(8,128)S(1)} %get-tuple-element.15.item_ref), custom_call_target="tpu_custom_call" | custom-call | tf_op jit(solution)/shard_map/other_items/pallas_call | solution.py:265
  23.2 4.1 %all-gather = bf16[32,64,128]{2,1,0:T(8,128)(2,1)S(1)} all-gather(bf16[16,64,128]{2,1,0:T(8,128)(2,1)S(1)} %get-tuple-element.17), channel_id=2, replica_groups={{0,1},{2,3},{4,5},{6,7},{8,9},{10,11},{12,13},{14,15},{16,17},{18,19},{..., dimensions={0}, use_global_device_ids=true | all-gather | bytes 786432 | tf_op jit(solution)/shard_map/all_gather | solution.py:298
  27.3 0.1 first_terms.1
  27.4 23.2 %all_to_all.15.parts_ref = bf16[16,64,128]{2,1,0:T(8,128)(2,1)S(1)} all-to-all(bf16[16,64,128]{2,1,0:T(8,128)(2,1)S(1)} %first_terms.1), channel_id=1, replica_groups={{0,2,4,6,8,10,12,14,16,18,20,22,24,26,28,30},{32,34,36,38,40,42,44,46,4..., dimensions={0} | all-to-all | bytes 524288 | tf_op jit(solution)/shard_map/all_to_all | solution.py:300
  50.5 0.1 second_terms.1
  50.6 14.2 %all_to_all.16 = bf16[16,64,128]{2,1,0:T(8,128)(2,1)S(1)} all-to-all(bf16[16,64,128]{2,1,0:T(8,128)(2,1)S(1)} %get-tuple-element.19), channel_id=1, replica_groups={{0,2,4,6,8,10,12,14,16,18,20,22,24,26,28,30},{32,34,36,38,40,42,44,46,4..., dimensions={0} | all-to-all | bytes 524288 | tf_op jit(solution)/shard_map/all_to_all | solution.py:304
  64.8 2.2 %all-gather.1 = bf16[32,64,128]{2,1,0:T(8,128)(2,1)S(1)} all-gather(bf16[16,64,128]{2,1,0:T(8,128)(2,1)S(1)} %all_to_all.16), channel_id=3, replica_groups={{0,1},{2,3},{4,5},{6,7},{8,9},{10,11},{12,13},{14,15},{16,17},{18,19},{..., dimensions={0}, use_global_device_ids=true | all-gather | bytes 786432 | tf_op jit(solution)/shard_map/all_gather | solution.py:305
  67.0 0.8 %finish.1 = (f32[64,128]{1,0:T(8,128)}, f32[512,128]{1,0:T(8,128)}) custom-call(f32[64,128]{1,0:T(8,128)S(1)} %get-tuple-element.18.new_ref, bf16[2,16,64,128]{3,2,1,0:T(8,128)(2,1)S(1)} %bitcast.4), custom_call_target="tpu_custom_call" | custom-call | tf_op jit(solution)/shard_map/finish/pallas_call | solution.py:265
Async XLA Ops:
  2.2 18.3 %all-to-all-start = ((bf16[16,64,128]{2,1,0:T(8,128)(2,1)}), bf16[16,64,128]{2,1,0:T(8,128)(2,1)S(1)}, u32[]{:S(2)}, u32[]{:S(2)}) async-start(bf16[16,64,128]{2,1,0:T(8,128)(2,1)} %user_copies.1), calls=%async_computation | async-start | bytes 524288 | tf_op jit(solution)/shard_map/all_to_all | solution.py:289
  15.5 6.4 %collective-permute-start = (bf16[18,64,512]{2,1,0:T(8,128)(2,1)S(1)}, bf16[18,64,512]{2,1,0:T(8,128)(2,1)S(1)}, u32[]{:S(2)}, u32[]{:S(2)}) collective-permute-start(bf16[18,64,512]{2,1,0:T(8,128)(2,1)S(1)} %get-tuple-element.11.sent_ref), channel_id=1, source_target_pairs={{0,1},{1,0},{2,3},{3,2},{4,5},{5,4},{6,7},{7,6},{8,9},{9,8},{10,11... | collective-permute-start | bytes 3538952 | tf_op jit(solution)/shard_map/ppermute | solution.py:291
